TPU v7x, 256 devices: a whole 4x4x8 slice. The times are simulated.
256 devices in a mesh: sector: 64 (over x, y_hi, z), slab: 4 (over y_lo, core).
Axes of the slice: x: 4, y: 4 (y_hi: 2, y_lo: 2; y = y_hi * 2 + y_lo), z: 8, core: 2. Of those that a mesh axis runs over, the one named last changes fastest.
Arguments:
- measured: float32 [64, 262144], P('slab', 'sector'), may hold values from -64 to 64
- tof: bfloat16 [512, 16, 2, 128, 128], P('sector'), may hold values from -0.1875 to 0.1875
- tof_rows: int32 [512, 16, 2], P('sector'), may hold values from 0 to 31
- tile_owner: int32 [64], replicated, may hold values from 0 to 63, each once
Outputs:
- image: float32 [64, 131072], P('slab', 'sector')
- data_dual: float32 [64, 262144], P('slab', 'sector')
- wavelet_dual: float32 [64, 131072], P('slab', 'sector')
Inputs may be any that keep to these rules, and one draw needn't show every extreme that they name: `tile_owner`: each tile 0 to 63 is named exactly once.
All inputs are finite; a program needn't handle non-finite values.
Results may differ from a plain program's by a relative error of at most 0.0035.
Values may be sent and summed in bfloat16 or wider, within the bound.
A program may use at most 128 MiB of HBM per device.

v0:
```python
import jax
import jax.numpy as jnp
from jax import lax
from jax.sharding import PartitionSpec as P

ITERS = 3
dual_step = 0.5
primal_step = 0.15
wave_limit = 0.5
depth_limit = 0.5


def shifted(shard, axis, by):
    length = lax.axis_size(axis)
    return lax.ppermute(shard, axis, [(i, (i + by) % length) for i in range(length)])


def passed_along(block, axis, distance):
    devices = range(lax.axis_size(axis))
    route = [(i - distance, i) for i in devices if i - distance in devices]
    return lax.ppermute(block, axis, route)


def haar_pairs(upper_row, lower_row):
    sum_up = upper_row[..., 0] + upper_row[..., 1]
    dif_up = upper_row[..., 0] - upper_row[..., 1]
    sum_low = lower_row[..., 0] + lower_row[..., 1]
    dif_low = lower_row[..., 0] - lower_row[..., 1]
    top_row = jnp.stack([(sum_up + sum_low) * 0.5, (dif_up + dif_low) * 0.5], -1)
    low_row = jnp.stack([(sum_up - sum_low) * 0.5, (dif_up - dif_low) * 0.5], -1)
    return (top_row, low_row)


def body(measured, tof, tof_rows, tile_owner):
    stops = tof.shape[0]
    blocks = tof.shape[1]
    slots = tof.shape[2]
    width = tof.shape[3]
    depth_rows = measured.shape[0]
    time_blocks = measured.shape[1] // width
    pixels = blocks * width
    sectors = lax.axis_size("sector")
    band = pixels // sectors
    half = stops // 2
    flat_rows = tof_rows.reshape(-1)
    one_hot = (flat_rows[None, :] == jnp.arange(time_blocks, dtype=jnp.int32)[:, None]).astype(
        jnp.bfloat16
    )
    inverse = jnp.argsort(tile_owner)
    last_slab = lax.axis_index("slab") == lax.axis_size("slab") - 1
    row_ids = jnp.arange(depth_rows, dtype=jnp.int32)[:, None]
    keep_rows = jnp.logical_not(jnp.logical_and(last_slab, row_ids == depth_rows - 1))

    def contribute(piece, stop_at):
        shaped = piece.reshape(depth_rows, blocks, width)
        terms = jnp.einsum(
            "dbp,bkrp->dbkr", shaped, tof[stop_at], preferred_element_type=jnp.float32
        )
        return terms.reshape(depth_rows, blocks * slots, width)

    def pull(dual_half, stop_at):
        picked = dual_half.reshape(depth_rows, time_blocks, width)[:, tof_rows[stop_at]]
        gathered = jnp.einsum(
            "dbkr,bkrp->dbp", picked, tof[stop_at], preferred_element_type=jnp.float32
        )
        return gathered.reshape(depth_rows, pixels)

    def haar_tiles(tiles):
        shaped = tiles.reshape(depth_rows, sectors // 2, 2, band // 2, 2)
        top_row, low_row = haar_pairs(shaped[:, :, 0], shaped[:, :, 1])
        return jnp.stack([top_row, low_row], 2).reshape(depth_rows, pixels)

    image = jnp.zeros((depth_rows, pixels), jnp.float32)
    xbar = jnp.zeros((depth_rows, pixels), jnp.float32)
    depth_dual = jnp.zeros((depth_rows, pixels), jnp.float32)
    wavelet_dual = jnp.zeros((depth_rows, pixels), jnp.float32)
    data_dual = jnp.zeros(measured.shape, jnp.float32)
    for iteration in range(ITERS):
        forward_terms = [None] * stops
        current = shifted(xbar.astype(jnp.bfloat16), "sector", half)
        forward_terms[0] = contribute(current, 0)
        for forward_stop_at in range(1, stops):
            current = shifted(current, "sector", -1)
            forward_terms[forward_stop_at] = contribute(current, forward_stop_at)
        joined = jnp.concatenate(forward_terms, 1)
        high_part = joined.astype(jnp.bfloat16)
        low_part = (joined - high_part.astype(jnp.float32)).astype(jnp.bfloat16)
        summed = jnp.einsum("tn,dnr->dtr", one_hot, high_part, preferred_element_type=jnp.float32)
        summed = summed + jnp.einsum(
            "tn,dnr->dtr", one_hot, low_part, preferred_element_type=jnp.float32
        )
        forward_data = summed.reshape(depth_rows, time_blocks * width)
        data_dual = (data_dual + dual_step * (forward_data - measured)) / (1.0 + dual_step)
        outgoing = xbar.reshape(depth_rows, sectors, band)[:, inverse, :]
        tiles = lax.all_to_all(outgoing, "sector", split_axis=1, concat_axis=1, tiled=True).reshape(
            depth_rows, pixels
        )
        wavelet_dual = jnp.clip(
            wavelet_dual + dual_step * haar_tiles(tiles), -wave_limit, wave_limit
        )
        next_row = passed_along(xbar[:1], "slab", -1)
        diff = jnp.concatenate([xbar[1:], next_row], 0) - xbar
        depth_dual = jnp.clip(
            depth_dual + dual_step * jnp.where(keep_rows, diff, 0.0), -depth_limit, depth_limit
        )
        adjoint_dual_half = data_dual.astype(jnp.bfloat16)
        carried = pull(adjoint_dual_half, stops - 1)
        for adjoint_stop_at in range(stops - 2, -1, -1):
            carried = shifted(carried, "sector", 1) + pull(adjoint_dual_half, adjoint_stop_at)
        result = shifted(carried, "sector", -half)
        coeffs = haar_tiles(wavelet_dual).reshape(depth_rows, sectors, band)
        returned = lax.all_to_all(
            coeffs.astype(jnp.bfloat16), "sector", split_axis=1, concat_axis=1, tiled=True
        ).astype(coeffs.dtype)
        wave_back = returned[:, tile_owner, :].reshape(depth_rows, pixels)
        prev_row = passed_along(depth_dual[-1:], "slab", 1)
        update = result + wave_back + (jnp.concatenate([prev_row, depth_dual[:-1]], 0) - depth_dual)
        image_new = jnp.maximum(image - primal_step * update, 0.0)
        xbar = 2.0 * image_new - image
        image = image_new
    return (image, data_dual, wavelet_dual)


def solution(mesh):
    return jax.shard_map(
        body,
        mesh=mesh,
        in_specs=(
            P("slab", "sector"),
            P("sector", None, None, None, None),
            P("sector", None, None),
            P(),
        ),
        out_specs=(P("slab", "sector"), P("slab", "sector"), P("slab", "sector")),
        check_vma=False,
    )
```

profile of v0, /device:TPU:8, one launch (start us, length us, event | category | flops | bytes accessed | tf_op | source)
XLA Modules:
  0.0 654.0 jit_solution(3445373541841408756)
XLA Ops:
  0.6 7.3 %collective-permute-start = (bf16[16,2048]{1,0:T(8,128)(2,1)S(1)}, bf16[16,2048]{1,0:T(8,128)(2,1)S(1)}, u32[]{:S(2)}, u32[]{:S(2)}) collective-permute-start(bf16[16,2048]{1,0:T(8,128)(2,1)S(1)} %convert_element_type.67), channel_id=1, source_target_pairs={{0,16},{4,20},{8,24},{12,28},{16,32},{20,36},{24,40},{28,44},{32,4... | collective-permute-start | bytes 196616 | tf_op jit(solution)/shard_map/ppermute | solution.py:15
  13.5 8.4 %all-to-all-start = ((f32[64,1,512]{2,1,0:T(1,128)}), f32[64,1,512]{2,1,0:T(1,128)S(1)}, u32[]{:S(2)}, u32[]{:S(2)}) async-start(f32[64,1,512]{2,1,0:T(1,128)} %reshape.942), calls=%async_computation | async-start | bytes 262144 | tf_op jit(solution)/shard_map/all_to_all | solution.py:95
  33.6 7.6 %collective-permute-start.1 = (bf16[16,2048]{1,0:T(8,128)(2,1)S(1)}, bf16[16,2048]{1,0:T(8,128)(2,1)S(1)}, u32[]{:S(2)}, u32[]{:S(2)}) collective-permute-start(bf16[16,2048]{1,0:T(8,128)(2,1)S(1)} %collective-permute-done), channel_id=1, source_target_pairs={{0,252},{4,0},{8,4},{12,8},{16,12},{20,16},{24,20},{28,24},{32,28}... | collective-permute-start | bytes 196616 | tf_op jit(solution)/shard_map/ppermute | solution.py:15
  44.7 8.1 %collective-permute-start.2 = (bf16[16,2048]{1,0:T(8,128)(2,1)S(1)}, bf16[16,2048]{1,0:T(8,128)(2,1)}, u32[]{:S(2)}, u32[]{:S(2)}) collective-permute-start(bf16[16,2048]{1,0:T(8,128)(2,1)S(1)} %collective-permute-done.1), channel_id=1, source_target_pairs={{0,252},{4,0},{8,4},{12,8},{16,12},{20,16},{24,20},{28,24},{32,28}... | collective-permute-start | bytes 196616 | tf_op jit(solution)/shard_map/ppermute | solution.py:15
  57.2 8.2 %collective-permute-start.3 = (bf16[16,2048]{1,0:T(8,128)(2,1)}, bf16[16,2048]{1,0:T(8,128)(2,1)}, u32[]{:S(2)}, u32[]{:S(2)}) collective-permute-start(bf16[16,2048]{1,0:T(8,128)(2,1)} %collective-permute-done.2), channel_id=1, source_target_pairs={{0,252},{4,0},{8,4},{12,8},{16,12},{20,16},{24,20},{28,24},{32,28}... | collective-permute-start | bytes 196616 | tf_op jit(solution)/shard_map/ppermute | solution.py:15
  83.7 7.6 %collective-permute-start.4 = (bf16[16,2048]{1,0:T(8,128)(2,1)}, bf16[16,2048]{1,0:T(8,128)(2,1)S(1)}, u32[]{:S(2)}, u32[]{:S(2)}) collective-permute-start(bf16[16,2048]{1,0:T(8,128)(2,1)} %collective-permute-done.3), channel_id=1, source_target_pairs={{0,252},{4,0},{8,4},{12,8},{16,12},{20,16},{24,20},{28,24},{32,28}... | collective-permute-start | bytes 196616 | tf_op jit(solution)/shard_map/ppermute | solution.py:15
  95.2 8.3 %collective-permute-start.5 = (bf16[16,2048]{1,0:T(8,128)(2,1)S(1)}, bf16[16,2048]{1,0:T(8,128)(2,1)S(1)}, u32[]{:S(2)}, u32[]{:S(2)}) collective-permute-start(bf16[16,2048]{1,0:T(8,128)(2,1)S(1)} %collective-permute-done.4), channel_id=1, source_target_pairs={{0,252},{4,0},{8,4},{12,8},{16,12},{20,16},{24,20},{28,24},{32,28}... | collective-permute-start | bytes 196616 | tf_op jit(solution)/shard_map/ppermute | solution.py:15
  107.0 8.1 %collective-permute-start.6 = (bf16[16,2048]{1,0:T(8,128)(2,1)S(1)}, bf16[16,2048]{1,0:T(8,128)(2,1)S(1)}, u32[]{:S(2)}, u32[]{:S(2)}) collective-permute-start(bf16[16,2048]{1,0:T(8,128)(2,1)S(1)} %collective-permute-done.5), channel_id=1, source_target_pairs={{0,252},{4,0},{8,4},{12,8},{16,12},{20,16},{24,20},{28,24},{32,28}... | collective-permute-start | bytes 196616 | tf_op jit(solution)/shard_map/ppermute | solution.py:15
  118.6 8.1 %collective-permute-start.7 = (bf16[16,2048]{1,0:T(8,128)(2,1)S(1)}, bf16[16,2048]{1,0:T(8,128)(2,1)S(1)}, u32[]{:S(2)}, u32[]{:S(2)}) collective-permute-start(bf16[16,2048]{1,0:T(8,128)(2,1)S(1)} %collective-permute-done.6), channel_id=1, source_target_pairs={{0,252},{4,0},{8,4},{12,8},{16,12},{20,16},{24,20},{28,24},{32,28}... | collective-permute-start | bytes 196616 | tf_op jit(solution)/shard_map/ppermute | solution.py:15
  146.5 10.3 %collective-permute-done.9 = f32[16,2048]{1,0:T(8,128)S(1)} collective-permute-done((f32[16,2048]{1,0:T(8,128)S(1)}, f32[16,2048]{1,0:T(8,128)S(1)}, u32[]{:S(2)}, u32[]{:S(2)}) %collective-permute-start.9) | collective-permute-done | bytes 131104 | tf_op jit(solution)/shard_map/ppermute | solution.py:15
  158.4 9.5 %collective-permute-done.10 = f32[16,2048]{1,0:T(8,128)S(1)} collective-permute-done((f32[16,2048]{1,0:T(8,128)S(1)}, f32[16,2048]{1,0:T(8,128)S(1)}, u32[]{:S(2)}, u32[]{:S(2)}) %collective-permute-start.10) | collective-permute-done | bytes 131104 | tf_op jit(solution)/shard_map/ppermute | solution.py:15
  169.4 9.2 %collective-permute-done.11 = f32[16,2048]{1,0:T(8,128)S(1)} collective-permute-done((f32[16,2048]{1,0:T(8,128)S(1)}, f32[16,2048]{1,0:T(8,128)S(1)}, u32[]{:S(2)}, u32[]{:S(2)}) %collective-permute-start.11) | collective-permute-done | bytes 131104 | tf_op jit(solution)/shard_map/ppermute | solution.py:15
  180.2 9.2 %collective-permute-done.12 = f32[16,2048]{1,0:T(8,128)S(1)} collective-permute-done((f32[16,2048]{1,0:T(8,128)S(1)}, f32[16,2048]{1,0:T(8,128)S(1)}, u32[]{:S(2)}, u32[]{:S(2)}) %collective-permute-start.12) | collective-permute-done | bytes 131104 | tf_op jit(solution)/shard_map/ppermute | solution.py:15
  191.0 9.2 %collective-permute-done.13 = f32[16,2048]{1,0:T(8,128)S(1)} collective-permute-done((f32[16,2048]{1,0:T(8,128)S(1)}, f32[16,2048]{1,0:T(8,128)S(1)}, u32[]{:S(2)}, u32[]{:S(2)}) %collective-permute-start.13) | collective-permute-done | bytes 131104 | tf_op jit(solution)/shard_map/ppermute | solution.py:15
  201.8 9.2 %collective-permute-done.14 = f32[16,2048]{1,0:T(8,128)S(1)} collective-permute-done((f32[16,2048]{1,0:T(8,128)S(1)}, f32[16,2048]{1,0:T(8,128)S(1)}, u32[]{:S(2)}, u32[]{:S(2)}) %collective-permute-start.14) | collective-permute-done | bytes 131104 | tf_op jit(solution)/shard_map/ppermute | solution.py:15
  212.8 7.6 %collective-permute-done.15 = f32[16,2048]{1,0:T(8,128)S(1)} collective-permute-done((f32[16,2048]{1,0:T(8,128)S(1)}, f32[16,2048]{1,0:T(8,128)S(1)}, u32[]{:S(2)}, u32[]{:S(2)}) %collective-permute-start.15) | collective-permute-done | bytes 131104 | tf_op jit(solution)/shard_map/ppermute | solution.py:15
  225.4 6.8 %all-to-all-start.2 = ((f32[64,1,512]{2,1,0:T(1,128)}), f32[64,1,512]{2,1,0:T(1,128)S(1)}, u32[]{:S(2)}, u32[]{:S(2)}) async-start(f32[64,1,512]{2,1,0:T(1,128)} %reshape.946), calls=%async_computation.2 | async-start | bytes 262144 | tf_op jit(solution)/shard_map/all_to_all | solution.py:95
  240.4 8.3 %collective-permute-done.18 = bf16[16,2048]{1,0:T(8,128)(2,1)S(1)} collective-permute-done((bf16[16,2048]{1,0:T(8,128)(2,1)S(1)}, bf16[16,2048]{1,0:T(8,128)(2,1)S(1)}, u32[]{:S(2)}, u32[]{:S(2)}) %collective-permute-start.18) | collective-permute-done | bytes 65568 | tf_op jit(solution)/shard_map/ppermute | solution.py:15
  256.3 6.1 collective-permute-start.20
  266.7 8.2 %collective-permute-start.21 = (bf16[16,2048]{1,0:T(8,128)(2,1)}, bf16[16,2048]{1,0:T(8,128)(2,1)}, u32[]{:S(2)}, u32[]{:S(2)}) collective-permute-start(bf16[16,2048]{1,0:T(8,128)(2,1)} %collective-permute-done.20), channel_id=1, source_target_pairs={{0,252},{4,0},{8,4},{12,8},{16,12},{20,16},{24,20},{28,24},{32,28}... | collective-permute-start | bytes 196616 | tf_op jit(solution)/shard_map/ppermute | solution.py:15
  293.9 7.7 %collective-permute-start.22 = (bf16[16,2048]{1,0:T(8,128)(2,1)}, bf16[16,2048]{1,0:T(8,128)(2,1)S(1)}, u32[]{:S(2)}, u32[]{:S(2)}) collective-permute-start(bf16[16,2048]{1,0:T(8,128)(2,1)} %collective-permute-done.21), channel_id=1, source_target_pairs={{0,252},{4,0},{8,4},{12,8},{16,12},{20,16},{24,20},{28,24},{32,28}... | collective-permute-start | bytes 196616 | tf_op jit(solution)/shard_map/ppermute | solution.py:15
  305.4 8.2 %collective-permute-start.23 = (bf16[16,2048]{1,0:T(8,128)(2,1)S(1)}, bf16[16,2048]{1,0:T(8,128)(2,1)S(1)}, u32[]{:S(2)}, u32[]{:S(2)}) collective-permute-start(bf16[16,2048]{1,0:T(8,128)(2,1)S(1)} %collective-permute-done.22), channel_id=1, source_target_pairs={{0,252},{4,0},{8,4},{12,8},{16,12},{20,16},{24,20},{28,24},{32,28}... | collective-permute-start | bytes 196616 | tf_op jit(solution)/shard_map/ppermute | solution.py:15
  317.1 8.1 %collective-permute-start.24 = (bf16[16,2048]{1,0:T(8,128)(2,1)S(1)}, bf16[16,2048]{1,0:T(8,128)(2,1)S(1)}, u32[]{:S(2)}, u32[]{:S(2)}) collective-permute-start(bf16[16,2048]{1,0:T(8,128)(2,1)S(1)} %collective-permute-done.23), channel_id=1, source_target_pairs={{0,252},{4,0},{8,4},{12,8},{16,12},{20,16},{24,20},{28,24},{32,28}... | collective-permute-start | bytes 196616 | tf_op jit(solution)/shard_map/ppermute | solution.py:15
  328.7 8.1 %collective-permute-start.25 = (bf16[16,2048]{1,0:T(8,128)(2,1)S(1)}, bf16[16,2048]{1,0:T(8,128)(2,1)S(1)}, u32[]{:S(2)}, u32[]{:S(2)}) collective-permute-start(bf16[16,2048]{1,0:T(8,128)(2,1)S(1)} %collective-permute-done.24), channel_id=1, source_target_pairs={{0,252},{4,0},{8,4},{12,8},{16,12},{20,16},{24,20},{28,24},{32,28}... | collective-permute-start | bytes 196616 | tf_op jit(solution)/shard_map/ppermute | solution.py:15
  350.1 10.3 %collective-permute-done.26 = f32[16,2048]{1,0:T(8,128)S(1)} collective-permute-done((f32[16,2048]{1,0:T(8,128)S(1)}, f32[16,2048]{1,0:T(8,128)S(1)}, u32[]{:S(2)}, u32[]{:S(2)}) %collective-permute-start.26) | collective-permute-done | bytes 131104 | tf_op jit(solution)/shard_map/ppermute | solution.py:15
  362.0 10.1 %collective-permute-done.27 = f32[16,2048]{1,0:T(8,128)S(1)} collective-permute-done((f32[16,2048]{1,0:T(8,128)S(1)}, f32[16,2048]{1,0:T(8,128)S(1)}, u32[]{:S(2)}, u32[]{:S(2)}) %collective-permute-start.27) | collective-permute-done | bytes 131104 | tf_op jit(solution)/shard_map/ppermute | solution.py:15
  373.7 9.4 %collective-permute-done.28 = f32[16,2048]{1,0:T(8,128)S(1)} collective-permute-done((f32[16,2048]{1,0:T(8,128)S(1)}, f32[16,2048]{1,0:T(8,128)S(1)}, u32[]{:S(2)}, u32[]{:S(2)}) %collective-permute-start.28) | collective-permute-done | bytes 131104 | tf_op jit(solution)/shard_map/ppermute | solution.py:15
  384.6 9.2 %collective-permute-done.29 = f32[16,2048]{1,0:T(8,128)S(1)} collective-permute-done((f32[16,2048]{1,0:T(8,128)S(1)}, f32[16,2048]{1,0:T(8,128)S(1)}, u32[]{:S(2)}, u32[]{:S(2)}) %collective-permute-start.29) | collective-permute-done | bytes 131104 | tf_op jit(solution)/shard_map/ppermute | solution.py:15
  395.4 9.2 %collective-permute-done.30 = f32[16,2048]{1,0:T(8,128)S(1)} collective-permute-done((f32[16,2048]{1,0:T(8,128)S(1)}, f32[16,2048]{1,0:T(8,128)S(1)}, u32[]{:S(2)}, u32[]{:S(2)}) %collective-permute-start.30) | collective-permute-done | bytes 131104 | tf_op jit(solution)/shard_map/ppermute | solution.py:15
  406.2 9.2 %collective-permute-done.31 = f32[16,2048]{1,0:T(8,128)S(1)} collective-permute-done((f32[16,2048]{1,0:T(8,128)S(1)}, f32[16,2048]{1,0:T(8,128)S(1)}, u32[]{:S(2)}, u32[]{:S(2)}) %collective-permute-start.31) | collective-permute-done | bytes 131104 | tf_op jit(solution)/shard_map/ppermute | solution.py:15
  417.0 9.2 %collective-permute-done.32 = f32[16,2048]{1,0:T(8,128)S(1)} collective-permute-done((f32[16,2048]{1,0:T(8,128)S(1)}, f32[16,2048]{1,0:T(8,128)S(1)}, u32[]{:S(2)}, u32[]{:S(2)}) %collective-permute-start.32) | collective-permute-done | bytes 131104 | tf_op jit(solution)/shard_map/ppermute | solution.py:15
  427.8 7.6 %collective-permute-done.33 = f32[16,2048]{1,0:T(8,128)S(1)} collective-permute-done((f32[16,2048]{1,0:T(8,128)S(1)}, f32[16,2048]{1,0:T(8,128)S(1)}, u32[]{:S(2)}, u32[]{:S(2)}) %collective-permute-start.33) | collective-permute-done | bytes 131104 | tf_op jit(solution)/shard_map/ppermute | solution.py:15
  441.0 6.8 %all-to-all-start.4 = ((f32[64,1,512]{2,1,0:T(1,128)}), f32[64,1,512]{2,1,0:T(1,128)S(1)}, u32[]{:S(2)}, u32[]{:S(2)}) async-start(f32[64,1,512]{2,1,0:T(1,128)} %reshape.950), calls=%async_computation.4 | async-start | bytes 262144 | tf_op jit(solution)/shard_map/all_to_all | solution.py:95
  456.0 8.3 %collective-permute-done.36 = bf16[16,2048]{1,0:T(8,128)(2,1)S(1)} collective-permute-done((bf16[16,2048]{1,0:T(8,128)(2,1)S(1)}, bf16[16,2048]{1,0:T(8,128)(2,1)S(1)}, u32[]{:S(2)}, u32[]{:S(2)}) %collective-permute-start.36) | collective-permute-done | bytes 65568 | tf_op jit(solution)/shard_map/ppermute | solution.py:15
  471.8 6.1 collective-permute-start.38
  481.4 8.1 %collective-permute-start.39 = (bf16[16,2048]{1,0:T(8,128)(2,1)S(1)}, bf16[16,2048]{1,0:T(8,128)(2,1)S(1)}, u32[]{:S(2)}, u32[]{:S(2)}) collective-permute-start(bf16[16,2048]{1,0:T(8,128)(2,1)S(1)} %collective-permute-done.38), channel_id=1, source_target_pairs={{0,252},{4,0},{8,4},{12,8},{16,12},{20,16},{24,20},{28,24},{32,28}... | collective-permute-start | bytes 196616 | tf_op jit(solution)/shard_map/ppermute | solution.py:15
  511.0 8.1 %collective-permute-start.40 = (bf16[16,2048]{1,0:T(8,128)(2,1)S(1)}, bf16[16,2048]{1,0:T(8,128)(2,1)S(1)}, u32[]{:S(2)}, u32[]{:S(2)}) collective-permute-start(bf16[16,2048]{1,0:T(8,128)(2,1)S(1)} %collective-permute-done.39), channel_id=1, source_target_pairs={{0,252},{4,0},{8,4},{12,8},{16,12},{20,16},{24,20},{28,24},{32,28}... | collective-permute-start | bytes 196616 | tf_op jit(solution)/shard_map/ppermute | solution.py:15
  522.6 8.1 %collective-permute-start.41 = (bf16[16,2048]{1,0:T(8,128)(2,1)S(1)}, bf16[16,2048]{1,0:T(8,128)(2,1)S(1)}, u32[]{:S(2)}, u32[]{:S(2)}) collective-permute-start(bf16[16,2048]{1,0:T(8,128)(2,1)S(1)} %collective-permute-done.40), channel_id=1, source_target_pairs={{0,252},{4,0},{8,4},{12,8},{16,12},{20,16},{24,20},{28,24},{32,28}... | collective-permute-start | bytes 196616 | tf_op jit(solution)/shard_map/ppermute | solution.py:15
  534.2 8.1 %collective-permute-start.42 = (bf16[16,2048]{1,0:T(8,128)(2,1)S(1)}, bf16[16,2048]{1,0:T(8,128)(2,1)S(1)}, u32[]{:S(2)}, u32[]{:S(2)}) collective-permute-start(bf16[16,2048]{1,0:T(8,128)(2,1)S(1)} %collective-permute-done.41), channel_id=1, source_target_pairs={{0,252},{4,0},{8,4},{12,8},{16,12},{20,16},{24,20},{28,24},{32,28}... | collective-permute-start | bytes 196616 | tf_op jit(solution)/shard_map/ppermute | solution.py:15
  545.9 8.1 %collective-permute-start.43 = (bf16[16,2048]{1,0:T(8,128)(2,1)S(1)}, bf16[16,2048]{1,0:T(8,128)(2,1)S(1)}, u32[]{:S(2)}, u32[]{:S(2)}) collective-permute-start(bf16[16,2048]{1,0:T(8,128)(2,1)S(1)} %collective-permute-done.42), channel_id=1, source_target_pairs={{0,252},{4,0},{8,4},{12,8},{16,12},{20,16},{24,20},{28,24},{32,28}... | collective-permute-start | bytes 196616 | tf_op jit(solution)/shard_map/ppermute | solution.py:15
  567.4 10.3 %collective-permute-done.44 = f32[16,2048]{1,0:T(8,128)S(1)} collective-permute-done((f32[16,2048]{1,0:T(8,128)S(1)}, f32[16,2048]{1,0:T(8,128)S(1)}, u32[]{:S(2)}, u32[]{:S(2)}) %collective-permute-start.44) | collective-permute-done | bytes 131104 | tf_op jit(solution)/shard_map/ppermute | solution.py:15
  579.2 10.1 %collective-permute-done.45 = f32[16,2048]{1,0:T(8,128)S(1)} collective-permute-done((f32[16,2048]{1,0:T(8,128)S(1)}, f32[16,2048]{1,0:T(8,128)S(1)}, u32[]{:S(2)}, u32[]{:S(2)}) %collective-permute-start.45) | collective-permute-done | bytes 131104 | tf_op jit(solution)/shard_map/ppermute | solution.py:15
  591.0 9.4 %collective-permute-done.46 = f32[16,2048]{1,0:T(8,128)S(1)} collective-permute-done((f32[16,2048]{1,0:T(8,128)S(1)}, f32[16,2048]{1,0:T(8,128)S(1)}, u32[]{:S(2)}, u32[]{:S(2)}) %collective-permute-start.46) | collective-permute-done | bytes 131104 | tf_op jit(solution)/shard_map/ppermute | solution.py:15
  601.9 9.2 %collective-permute-done.47 = f32[16,2048]{1,0:T(8,128)S(1)} collective-permute-done((f32[16,2048]{1,0:T(8,128)S(1)}, f32[16,2048]{1,0:T(8,128)S(1)}, u32[]{:S(2)}, u32[]{:S(2)}) %collective-permute-start.47) | collective-permute-done | bytes 131104 | tf_op jit(solution)/shard_map/ppermute | solution.py:15
  612.7 9.2 %collective-permute-done.48 = f32[16,2048]{1,0:T(8,128)S(1)} collective-permute-done((f32[16,2048]{1,0:T(8,128)S(1)}, f32[16,2048]{1,0:T(8,128)S(1)}, u32[]{:S(2)}, u32[]{:S(2)}) %collective-permute-start.48) | collective-permute-done | bytes 131104 | tf_op jit(solution)/shard_map/ppermute | solution.py:15
  623.5 9.2 %collective-permute-done.49 = f32[16,2048]{1,0:T(8,128)S(1)} collective-permute-done((f32[16,2048]{1,0:T(8,128)S(1)}, f32[16,2048]{1,0:T(8,128)S(1)}, u32[]{:S(2)}, u32[]{:S(2)}) %collective-permute-start.49) | collective-permute-done | bytes 131104 | tf_op jit(solution)/shard_map/ppermute | solution.py:15
  634.3 9.2 %collective-permute-done.50 = f32[16,2048]{1,0:T(8,128)S(1)} collective-permute-done((f32[16,2048]{1,0:T(8,128)S(1)}, f32[16,2048]{1,0:T(8,128)S(1)}, u32[]{:S(2)}, u32[]{:S(2)}) %collective-permute-start.50) | collective-permute-done | bytes 131104 | tf_op jit(solution)/shard_map/ppermute | solution.py:15
  644.8 7.6 %collective-permute-done.51 = f32[16,2048]{1,0:T(8,128)S(1)} collective-permute-done((f32[16,2048]{1,0:T(8,128)S(1)}, f32[16,2048]{1,0:T(8,128)S(1)}, u32[]{:S(2)}, u32[]{:S(2)}) %collective-permute-start.51) | collective-permute-done | bytes 131104 | tf_op jit(solution)/shard_map/ppermute | solution.py:15
  (421 shorter events, 243.8 us)
Async XLA Ops:
  0.6 31.3 %collective-permute-start = (bf16[16,2048]{1,0:T(8,128)(2,1)S(1)}, bf16[16,2048]{1,0:T(8,128)(2,1)S(1)}, u32[]{:S(2)}, u32[]{:S(2)}) collective-permute-start(bf16[16,2048]{1,0:T(8,128)(2,1)S(1)} %convert_element_type.67), channel_id=1, source_target_pairs={{0,16},{4,20},{8,24},{12,28},{16,32},{20,36},{24,40},{28,44},{32,4... | collective-permute-start | bytes 196616 | tf_op jit(solution)/shard_map/ppermute | solution.py:15
  13.5 52.0 %all-to-all-start = ((f32[64,1,512]{2,1,0:T(1,128)}), f32[64,1,512]{2,1,0:T(1,128)S(1)}, u32[]{:S(2)}, u32[]{:S(2)}) async-start(f32[64,1,512]{2,1,0:T(1,128)} %reshape.942), calls=%async_computation | async-start | bytes 262144 | tf_op jit(solution)/shard_map/all_to_all | solution.py:95
  29.8 183.0 %collective-permute-start.17 = (f32[1,2048]{1,0:T(1,128)}, f32[1,2048]{1,0:T(1,128)}, u32[]{:S(2)}, u32[]{:S(2)}) collective-permute-start(f32[1,2048]{1,0:T(1,128)} %slice.405), channel_id=1, source_target_pairs={{0,1},{1,2},{2,3},{4,5},{5,6},{6,7},{8,9},{9,10},{10,11},{12,13},{... | collective-permute-start | bytes 24584 | tf_op jit(solution)/shard_map/ppermute | solution.py:21
  44.7 10.0 %collective-permute-start.2 = (bf16[16,2048]{1,0:T(8,128)(2,1)S(1)}, bf16[16,2048]{1,0:T(8,128)(2,1)}, u32[]{:S(2)}, u32[]{:S(2)}) collective-permute-start(bf16[16,2048]{1,0:T(8,128)(2,1)S(1)} %collective-permute-done.1), channel_id=1, source_target_pairs={{0,252},{4,0},{8,4},{12,8},{16,12},{20,16},{24,20},{28,24},{32,28}... | collective-permute-start | bytes 196616 | tf_op jit(solution)/shard_map/ppermute | solution.py:15
  57.2 24.1 %collective-permute-start.3 = (bf16[16,2048]{1,0:T(8,128)(2,1)}, bf16[16,2048]{1,0:T(8,128)(2,1)}, u32[]{:S(2)}, u32[]{:S(2)}) collective-permute-start(bf16[16,2048]{1,0:T(8,128)(2,1)} %collective-permute-done.2), channel_id=1, source_target_pairs={{0,252},{4,0},{8,4},{12,8},{16,12},{20,16},{24,20},{28,24},{32,28}... | collective-permute-start | bytes 196616 | tf_op jit(solution)/shard_map/ppermute | solution.py:15
  76.6 26.9 %all-to-all-start.1 = ((bf16[64,2,256]{2,1,0:T(2,128)(2,1)}), bf16[64,2,256]{2,1,0:T(2,128)(2,1)S(1)}, u32[]{:S(2)}, u32[]{:S(2)}) async-start(bf16[64,2,256]{2,1,0:T(2,128)(2,1)} %reshape.944), calls=%async_computation.1 | async-start | bytes 131072 | tf_op jit(solution)/shard_map/all_to_all | solution.py:112
  95.2 10.2 %collective-permute-start.5 = (bf16[16,2048]{1,0:T(8,128)(2,1)S(1)}, bf16[16,2048]{1,0:T(8,128)(2,1)S(1)}, u32[]{:S(2)}, u32[]{:S(2)}) collective-permute-start(bf16[16,2048]{1,0:T(8,128)(2,1)S(1)} %collective-permute-done.4), channel_id=1, source_target_pairs={{0,252},{4,0},{8,4},{12,8},{16,12},{20,16},{24,20},{28,24},{32,28}... | collective-permute-start | bytes 196616 | tf_op jit(solution)/shard_map/ppermute | solution.py:15
  107.0 10.0 %collective-permute-start.6 = (bf16[16,2048]{1,0:T(8,128)(2,1)S(1)}, bf16[16,2048]{1,0:T(8,128)(2,1)S(1)}, u32[]{:S(2)}, u32[]{:S(2)}) collective-permute-start(bf16[16,2048]{1,0:T(8,128)(2,1)S(1)} %collective-permute-done.5), channel_id=1, source_target_pairs={{0,252},{4,0},{8,4},{12,8},{16,12},{20,16},{24,20},{28,24},{32,28}... | collective-permute-start | bytes 196616 | tf_op jit(solution)/shard_map/ppermute | solution.py:15
  118.6 10.0 %collective-permute-start.7 = (bf16[16,2048]{1,0:T(8,128)(2,1)S(1)}, bf16[16,2048]{1,0:T(8,128)(2,1)S(1)}, u32[]{:S(2)}, u32[]{:S(2)}) collective-permute-start(bf16[16,2048]{1,0:T(8,128)(2,1)S(1)} %collective-permute-done.6), channel_id=1, source_target_pairs={{0,252},{4,0},{8,4},{12,8},{16,12},{20,16},{24,20},{28,24},{32,28}... | collective-permute-start | bytes 196616 | tf_op jit(solution)/shard_map/ppermute | solution.py:15
  133.2 11.7 %collective-permute-start.8 = (f32[16,2048]{1,0:T(8,128)S(1)}, f32[16,2048]{1,0:T(8,128)S(1)}, u32[]{:S(2)}, u32[]{:S(2)}) collective-permute-start(f32[16,2048]{1,0:T(8,128)S(1)} %bitcast.854), channel_id=1, source_target_pairs={{0,4},{4,8},{8,12},{12,16},{16,20},{20,24},{24,28},{28,32},{32,36}... | collective-permute-start | bytes 393224 | tf_op jit(solution)/shard_map/ppermute | solution.py:15
  144.9 11.9 %collective-permute-start.9 = (f32[16,2048]{1,0:T(8,128)S(1)}, f32[16,2048]{1,0:T(8,128)S(1)}, u32[]{:S(2)}, u32[]{:S(2)}) collective-permute-start(f32[16,2048]{1,0:T(8,128)S(1)} %bitcast_add_fusion.20), channel_id=1, source_target_pairs={{0,4},{4,8},{8,12},{12,16},{16,20},{20,24},{24,28},{28,32},{32,36}... | collective-permute-start | bytes 393224 | tf_op jit(solution)/shard_map/ppermute | solution.py:15
  156.8 11.0 %collective-permute-start.10 = (f32[16,2048]{1,0:T(8,128)S(1)}, f32[16,2048]{1,0:T(8,128)S(1)}, u32[]{:S(2)}, u32[]{:S(2)}) collective-permute-start(f32[16,2048]{1,0:T(8,128)S(1)} %bitcast_add_fusion.19), channel_id=1, source_target_pairs={{0,4},{4,8},{8,12},{12,16},{16,20},{20,24},{24,28},{28,32},{32,36}... | collective-permute-start | bytes 393224 | tf_op jit(solution)/shard_map/ppermute | solution.py:15
  167.9 10.8 %collective-permute-start.11 = (f32[16,2048]{1,0:T(8,128)S(1)}, f32[16,2048]{1,0:T(8,128)S(1)}, u32[]{:S(2)}, u32[]{:S(2)}) collective-permute-start(f32[16,2048]{1,0:T(8,128)S(1)} %bitcast_add_fusion.18), channel_id=1, source_target_pairs={{0,4},{4,8},{8,12},{12,16},{16,20},{20,24},{24,28},{28,32},{32,36}... | collective-permute-start | bytes 393224 | tf_op jit(solution)/shard_map/ppermute | solution.py:15
  178.6 10.8 %collective-permute-start.12 = (f32[16,2048]{1,0:T(8,128)S(1)}, f32[16,2048]{1,0:T(8,128)S(1)}, u32[]{:S(2)}, u32[]{:S(2)}) collective-permute-start(f32[16,2048]{1,0:T(8,128)S(1)} %bitcast_add_fusion.17), channel_id=1, source_target_pairs={{0,4},{4,8},{8,12},{12,16},{16,20},{20,24},{24,28},{28,32},{32,36}... | collective-permute-start | bytes 393224 | tf_op jit(solution)/shard_map/ppermute | solution.py:15
  189.4 10.8 %collective-permute-start.13 = (f32[16,2048]{1,0:T(8,128)S(1)}, f32[16,2048]{1,0:T(8,128)S(1)}, u32[]{:S(2)}, u32[]{:S(2)}) collective-permute-start(f32[16,2048]{1,0:T(8,128)S(1)} %bitcast_add_fusion.16), channel_id=1, source_target_pairs={{0,4},{4,8},{8,12},{12,16},{16,20},{20,24},{24,28},{28,32},{32,36}... | collective-permute-start | bytes 393224 | tf_op jit(solution)/shard_map/ppermute | solution.py:15
  200.2 10.8 %collective-permute-start.14 = (f32[16,2048]{1,0:T(8,128)S(1)}, f32[16,2048]{1,0:T(8,128)S(1)}, u32[]{:S(2)}, u32[]{:S(2)}) collective-permute-start(f32[16,2048]{1,0:T(8,128)S(1)} %bitcast_add_fusion.15), channel_id=1, source_target_pairs={{0,4},{4,8},{8,12},{12,16},{16,20},{20,24},{24,28},{28,32},{32,36}... | collective-permute-start | bytes 393224 | tf_op jit(solution)/shard_map/ppermute | solution.py:15
  222.5 15.3 %collective-permute-start.34 = (f32[1,2048]{1,0:T(1,128)S(1)}, f32[1,2048]{1,0:T(1,128)S(1)}, u32[]{:S(2)}, u32[]{:S(2)}) collective-permute-start(f32[1,2048]{1,0:T(1,128)S(1)} %slice.420), channel_id=1, source_target_pairs={{1,0},{2,1},{3,2},{5,4},{6,5},{7,6},{9,8},{10,9},{11,10},{13,12},{... | collective-permute-start | bytes 24584 | tf_op jit(solution)/shard_map/ppermute | solution.py:21
  225.4 49.6 %all-to-all-start.2 = ((f32[64,1,512]{2,1,0:T(1,128)}), f32[64,1,512]{2,1,0:T(1,128)S(1)}, u32[]{:S(2)}, u32[]{:S(2)}) async-start(f32[64,1,512]{2,1,0:T(1,128)} %reshape.946), calls=%async_computation.2 | async-start | bytes 262144 | tf_op jit(solution)/shard_map/all_to_all | solution.py:95
  232.2 16.5 %collective-permute-start.18 = (bf16[16,2048]{1,0:T(8,128)(2,1)S(1)}, bf16[16,2048]{1,0:T(8,128)(2,1)S(1)}, u32[]{:S(2)}, u32[]{:S(2)}) collective-permute-start(bf16[16,2048]{1,0:T(8,128)(2,1)S(1)} %get-tuple-element.19), channel_id=1, source_target_pairs={{0,16},{4,20},{8,24},{12,28},{16,32},{20,36},{24,40},{28,44},{32,4... | collective-permute-start | bytes 196616 | tf_op jit(solution)/shard_map/ppermute | solution.py:15
  238.5 189.3 %collective-permute-start.35 = (f32[1,2048]{1,0:T(1,128)}, f32[1,2048]{1,0:T(1,128)}, u32[]{:S(2)}, u32[]{:S(2)}) collective-permute-start(f32[1,2048]{1,0:T(1,128)} %slice.421), channel_id=1, source_target_pairs={{0,1},{1,2},{2,3},{4,5},{5,6},{6,7},{8,9},{9,10},{10,11},{12,13},{... | collective-permute-start | bytes 24584 | tf_op jit(solution)/shard_map/ppermute | solution.py:21
  266.7 24.7 %collective-permute-start.21 = (bf16[16,2048]{1,0:T(8,128)(2,1)}, bf16[16,2048]{1,0:T(8,128)(2,1)}, u32[]{:S(2)}, u32[]{:S(2)}) collective-permute-start(bf16[16,2048]{1,0:T(8,128)(2,1)} %collective-permute-done.20), channel_id=1, source_target_pairs={{0,252},{4,0},{8,4},{12,8},{16,12},{20,16},{24,20},{28,24},{32,28}... | collective-permute-start | bytes 196616 | tf_op jit(solution)/shard_map/ppermute | solution.py:15
  286.6 27.0 %all-to-all-start.3 = ((bf16[64,2,256]{2,1,0:T(2,128)(2,1)}), bf16[64,2,256]{2,1,0:T(2,128)(2,1)S(1)}, u32[]{:S(2)}, u32[]{:S(2)}) async-start(bf16[64,2,256]{2,1,0:T(2,128)(2,1)} %reshape.948), calls=%async_computation.3 | async-start | bytes 131072 | tf_op jit(solution)/shard_map/all_to_all | solution.py:112
  305.4 10.1 %collective-permute-start.23 = (bf16[16,2048]{1,0:T(8,128)(2,1)S(1)}, bf16[16,2048]{1,0:T(8,128)(2,1)S(1)}, u32[]{:S(2)}, u32[]{:S(2)}) collective-permute-start(bf16[16,2048]{1,0:T(8,128)(2,1)S(1)} %collective-permute-done.22), channel_id=1, source_target_pairs={{0,252},{4,0},{8,4},{12,8},{16,12},{20,16},{24,20},{28,24},{32,28}... | collective-permute-start | bytes 196616 | tf_op jit(solution)/shard_map/ppermute | solution.py:15
  317.1 10.0 %collective-permute-start.24 = (bf16[16,2048]{1,0:T(8,128)(2,1)S(1)}, bf16[16,2048]{1,0:T(8,128)(2,1)S(1)}, u32[]{:S(2)}, u32[]{:S(2)}) collective-permute-start(bf16[16,2048]{1,0:T(8,128)(2,1)S(1)} %collective-permute-done.23), channel_id=1, source_target_pairs={{0,252},{4,0},{8,4},{12,8},{16,12},{20,16},{24,20},{28,24},{32,28}... | collective-permute-start | bytes 196616 | tf_op jit(solution)/shard_map/ppermute | solution.py:15
  328.7 10.0 %collective-permute-start.25 = (bf16[16,2048]{1,0:T(8,128)(2,1)S(1)}, bf16[16,2048]{1,0:T(8,128)(2,1)S(1)}, u32[]{:S(2)}, u32[]{:S(2)}) collective-permute-start(bf16[16,2048]{1,0:T(8,128)(2,1)S(1)} %collective-permute-done.24), channel_id=1, source_target_pairs={{0,252},{4,0},{8,4},{12,8},{16,12},{20,16},{24,20},{28,24},{32,28}... | collective-permute-start | bytes 196616 | tf_op jit(solution)/shard_map/ppermute | solution.py:15
  348.6 11.8 %collective-permute-start.26 = (f32[16,2048]{1,0:T(8,128)S(1)}, f32[16,2048]{1,0:T(8,128)S(1)}, u32[]{:S(2)}, u32[]{:S(2)}) collective-permute-start(f32[16,2048]{1,0:T(8,128)S(1)} %bitcast.855), channel_id=1, source_target_pairs={{0,4},{4,8},{8,12},{12,16},{16,20},{20,24},{24,28},{28,32},{32,36}... | collective-permute-start | bytes 393224 | tf_op jit(solution)/shard_map/ppermute | solution.py:15
  360.4 11.7 %collective-permute-start.27 = (f32[16,2048]{1,0:T(8,128)S(1)}, f32[16,2048]{1,0:T(8,128)S(1)}, u32[]{:S(2)}, u32[]{:S(2)}) collective-permute-start(f32[16,2048]{1,0:T(8,128)S(1)} %bitcast_add_fusion.13), channel_id=1, source_target_pairs={{0,4},{4,8},{8,12},{12,16},{16,20},{20,24},{24,28},{28,32},{32,36}... | collective-permute-start | bytes 393224 | tf_op jit(solution)/shard_map/ppermute | solution.py:15
  372.1 10.9 %collective-permute-start.28 = (f32[16,2048]{1,0:T(8,128)S(1)}, f32[16,2048]{1,0:T(8,128)S(1)}, u32[]{:S(2)}, u32[]{:S(2)}) collective-permute-start(f32[16,2048]{1,0:T(8,128)S(1)} %bitcast_add_fusion.12), channel_id=1, source_target_pairs={{0,4},{4,8},{8,12},{12,16},{16,20},{20,24},{24,28},{28,32},{32,36}... | collective-permute-start | bytes 393224 | tf_op jit(solution)/shard_map/ppermute | solution.py:15
  383.1 10.8 %collective-permute-start.29 = (f32[16,2048]{1,0:T(8,128)S(1)}, f32[16,2048]{1,0:T(8,128)S(1)}, u32[]{:S(2)}, u32[]{:S(2)}) collective-permute-start(f32[16,2048]{1,0:T(8,128)S(1)} %bitcast_add_fusion.11), channel_id=1, source_target_pairs={{0,4},{4,8},{8,12},{12,16},{16,20},{20,24},{24,28},{28,32},{32,36}... | collective-permute-start | bytes 393224 | tf_op jit(solution)/shard_map/ppermute | solution.py:15
  393.9 10.8 %collective-permute-start.30 = (f32[16,2048]{1,0:T(8,128)S(1)}, f32[16,2048]{1,0:T(8,128)S(1)}, u32[]{:S(2)}, u32[]{:S(2)}) collective-permute-start(f32[16,2048]{1,0:T(8,128)S(1)} %bitcast_add_fusion.10), channel_id=1, source_target_pairs={{0,4},{4,8},{8,12},{12,16},{16,20},{20,24},{24,28},{28,32},{32,36}... | collective-permute-start | bytes 393224 | tf_op jit(solution)/shard_map/ppermute | solution.py:15
  404.6 10.8 %collective-permute-start.31 = (f32[16,2048]{1,0:T(8,128)S(1)}, f32[16,2048]{1,0:T(8,128)S(1)}, u32[]{:S(2)}, u32[]{:S(2)}) collective-permute-start(f32[16,2048]{1,0:T(8,128)S(1)} %bitcast_add_fusion.9), channel_id=1, source_target_pairs={{0,4},{4,8},{8,12},{12,16},{16,20},{20,24},{24,28},{28,32},{32,36}... | collective-permute-start | bytes 393224 | tf_op jit(solution)/shard_map/ppermute | solution.py:15
  415.4 10.8 %collective-permute-start.32 = (f32[16,2048]{1,0:T(8,128)S(1)}, f32[16,2048]{1,0:T(8,128)S(1)}, u32[]{:S(2)}, u32[]{:S(2)}) collective-permute-start(f32[16,2048]{1,0:T(8,128)S(1)} %bitcast_add_fusion.8), channel_id=1, source_target_pairs={{0,4},{4,8},{8,12},{12,16},{16,20},{20,24},{24,28},{28,32},{32,36}... | collective-permute-start | bytes 393224 | tf_op jit(solution)/shard_map/ppermute | solution.py:15
  438.1 15.3 %collective-permute-start.52 = (f32[1,2048]{1,0:T(1,128)S(1)}, f32[1,2048]{1,0:T(1,128)S(1)}, u32[]{:S(2)}, u32[]{:S(2)}) collective-permute-start(f32[1,2048]{1,0:T(1,128)S(1)} %slice.436), channel_id=1, source_target_pairs={{1,0},{2,1},{3,2},{5,4},{6,5},{7,6},{9,8},{10,9},{11,10},{13,12},{... | collective-permute-start | bytes 24584 | tf_op jit(solution)/shard_map/ppermute | solution.py:21
  441.0 48.6 %all-to-all-start.4 = ((f32[64,1,512]{2,1,0:T(1,128)}), f32[64,1,512]{2,1,0:T(1,128)S(1)}, u32[]{:S(2)}, u32[]{:S(2)}) async-start(f32[64,1,512]{2,1,0:T(1,128)} %reshape.950), calls=%async_computation.4 | async-start | bytes 262144 | tf_op jit(solution)/shard_map/all_to_all | solution.py:95
  447.8 16.5 %collective-permute-start.36 = (bf16[16,2048]{1,0:T(8,128)(2,1)S(1)}, bf16[16,2048]{1,0:T(8,128)(2,1)S(1)}, u32[]{:S(2)}, u32[]{:S(2)}) collective-permute-start(bf16[16,2048]{1,0:T(8,128)(2,1)S(1)} %get-tuple-element.16), channel_id=1, source_target_pairs={{0,16},{4,20},{8,24},{12,28},{16,32},{20,36},{24,40},{28,44},{32,4... | collective-permute-start | bytes 196616 | tf_op jit(solution)/shard_map/ppermute | solution.py:15
  454.0 190.8 %collective-permute-start.53 = (f32[1,2048]{1,0:T(1,128)}, f32[1,2048]{1,0:T(1,128)}, u32[]{:S(2)}, u32[]{:S(2)}) collective-permute-start(f32[1,2048]{1,0:T(1,128)} %slice.437), channel_id=1, source_target_pairs={{0,1},{1,2},{2,3},{4,5},{5,6},{6,7},{8,9},{9,10},{10,11},{12,13},{... | collective-permute-start | bytes 24584 | tf_op jit(solution)/shard_map/ppermute | solution.py:21
  481.4 28.0 %collective-permute-start.39 = (bf16[16,2048]{1,0:T(8,128)(2,1)S(1)}, bf16[16,2048]{1,0:T(8,128)(2,1)S(1)}, u32[]{:S(2)}, u32[]{:S(2)}) collective-permute-start(bf16[16,2048]{1,0:T(8,128)(2,1)S(1)} %collective-permute-done.38), channel_id=1, source_target_pairs={{0,252},{4,0},{8,4},{12,8},{16,12},{20,16},{24,20},{28,24},{32,28}... | collective-permute-start | bytes 196616 | tf_op jit(solution)/shard_map/ppermute | solution.py:15
  502.4 28.4 %all-to-all-start.5 = ((bf16[64,2,256]{2,1,0:T(2,128)(2,1)}), bf16[64,2,256]{2,1,0:T(2,128)(2,1)S(1)}, u32[]{:S(2)}, u32[]{:S(2)}) async-start(bf16[64,2,256]{2,1,0:T(2,128)(2,1)} %reshape.952), calls=%async_computation.5 | async-start | bytes 131072 | tf_op jit(solution)/shard_map/all_to_all | solution.py:112
  522.6 10.0 %collective-permute-start.41 = (bf16[16,2048]{1,0:T(8,128)(2,1)S(1)}, bf16[16,2048]{1,0:T(8,128)(2,1)S(1)}, u32[]{:S(2)}, u32[]{:S(2)}) collective-permute-start(bf16[16,2048]{1,0:T(8,128)(2,1)S(1)} %collective-permute-done.40), channel_id=1, source_target_pairs={{0,252},{4,0},{8,4},{12,8},{16,12},{20,16},{24,20},{28,24},{32,28}... | collective-permute-start | bytes 196616 | tf_op jit(solution)/shard_map/ppermute | solution.py:15
  534.2 10.0 %collective-permute-start.42 = (bf16[16,2048]{1,0:T(8,128)(2,1)S(1)}, bf16[16,2048]{1,0:T(8,128)(2,1)S(1)}, u32[]{:S(2)}, u32[]{:S(2)}) collective-permute-start(bf16[16,2048]{1,0:T(8,128)(2,1)S(1)} %collective-permute-done.41), channel_id=1, source_target_pairs={{0,252},{4,0},{8,4},{12,8},{16,12},{20,16},{24,20},{28,24},{32,28}... | collective-permute-start | bytes 196616 | tf_op jit(solution)/shard_map/ppermute | solution.py:15
  545.9 10.0 %collective-permute-start.43 = (bf16[16,2048]{1,0:T(8,128)(2,1)S(1)}, bf16[16,2048]{1,0:T(8,128)(2,1)S(1)}, u32[]{:S(2)}, u32[]{:S(2)}) collective-permute-start(bf16[16,2048]{1,0:T(8,128)(2,1)S(1)} %collective-permute-done.42), channel_id=1, source_target_pairs={{0,252},{4,0},{8,4},{12,8},{16,12},{20,16},{24,20},{28,24},{32,28}... | collective-permute-start | bytes 196616 | tf_op jit(solution)/shard_map/ppermute | solution.py:15
  565.8 11.8 %collective-permute-start.44 = (f32[16,2048]{1,0:T(8,128)S(1)}, f32[16,2048]{1,0:T(8,128)S(1)}, u32[]{:S(2)}, u32[]{:S(2)}) collective-permute-start(f32[16,2048]{1,0:T(8,128)S(1)} %bitcast.856), channel_id=1, source_target_pairs={{0,4},{4,8},{8,12},{12,16},{16,20},{20,24},{24,28},{28,32},{32,36}... | collective-permute-start | bytes 393224 | tf_op jit(solution)/shard_map/ppermute | solution.py:15
  577.7 11.7 %collective-permute-start.45 = (f32[16,2048]{1,0:T(8,128)S(1)}, f32[16,2048]{1,0:T(8,128)S(1)}, u32[]{:S(2)}, u32[]{:S(2)}) collective-permute-start(f32[16,2048]{1,0:T(8,128)S(1)} %bitcast_add_fusion.6), channel_id=1, source_target_pairs={{0,4},{4,8},{8,12},{12,16},{16,20},{20,24},{24,28},{28,32},{32,36}... | collective-permute-start | bytes 393224 | tf_op jit(solution)/shard_map/ppermute | solution.py:15
  589.4 10.9 %collective-permute-start.46 = (f32[16,2048]{1,0:T(8,128)S(1)}, f32[16,2048]{1,0:T(8,128)S(1)}, u32[]{:S(2)}, u32[]{:S(2)}) collective-permute-start(f32[16,2048]{1,0:T(8,128)S(1)} %bitcast_add_fusion.5), channel_id=1, source_target_pairs={{0,4},{4,8},{8,12},{12,16},{16,20},{20,24},{24,28},{28,32},{32,36}... | collective-permute-start | bytes 393224 | tf_op jit(solution)/shard_map/ppermute | solution.py:15
  600.3 10.8 %collective-permute-start.47 = (f32[16,2048]{1,0:T(8,128)S(1)}, f32[16,2048]{1,0:T(8,128)S(1)}, u32[]{:S(2)}, u32[]{:S(2)}) collective-permute-start(f32[16,2048]{1,0:T(8,128)S(1)} %bitcast_add_fusion.4), channel_id=1, source_target_pairs={{0,4},{4,8},{8,12},{12,16},{16,20},{20,24},{24,28},{28,32},{32,36}... | collective-permute-start | bytes 393224 | tf_op jit(solution)/shard_map/ppermute | solution.py:15
  611.1 10.8 %collective-permute-start.48 = (f32[16,2048]{1,0:T(8,128)S(1)}, f32[16,2048]{1,0:T(8,128)S(1)}, u32[]{:S(2)}, u32[]{:S(2)}) collective-permute-start(f32[16,2048]{1,0:T(8,128)S(1)} %bitcast_add_fusion.3), channel_id=1, source_target_pairs={{0,4},{4,8},{8,12},{12,16},{16,20},{20,24},{24,28},{28,32},{32,36}... | collective-permute-start | bytes 393224 | tf_op jit(solution)/shard_map/ppermute | solution.py:15
  621.9 10.8 %collective-permute-start.49 = (f32[16,2048]{1,0:T(8,128)S(1)}, f32[16,2048]{1,0:T(8,128)S(1)}, u32[]{:S(2)}, u32[]{:S(2)}) collective-permute-start(f32[16,2048]{1,0:T(8,128)S(1)} %bitcast_add_fusion.2), channel_id=1, source_target_pairs={{0,4},{4,8},{8,12},{12,16},{16,20},{20,24},{24,28},{28,32},{32,36}... | collective-permute-start | bytes 393224 | tf_op jit(solution)/shard_map/ppermute | solution.py:15
  632.7 10.8 %collective-permute-start.50 = (f32[16,2048]{1,0:T(8,128)S(1)}, f32[16,2048]{1,0:T(8,128)S(1)}, u32[]{:S(2)}, u32[]{:S(2)}) collective-permute-start(f32[16,2048]{1,0:T(8,128)S(1)} %bitcast_add_fusion.1), channel_id=1, source_target_pairs={{0,4},{4,8},{8,12},{12,16},{16,20},{20,24},{24,28},{28,32},{32,36}... | collective-permute-start | bytes 393224 | tf_op jit(solution)/shard_map/ppermute | solution.py:15
  (44 other events, 1544.6 us)
where the time goes:
time: 666 us; the launch traced here: 654 us
  waiting for transfers between devices  272 us (41%)
  starting transfers between devices  219 us (33%)
  matrix products  75.3 us (11%)
  local copies, waits for them, and re-layouts  66.8 us (10%)
  other arithmetic  18.5 us (3%)
    ppermute x48, waiting for transfers between devices, shifted(): lax.ppermute(shard, axis, [(i, (i + by) % length) for i in range(length)])  272 us
    ppermute x48, starting transfers between devices, shifted(): lax.ppermute(shard, axis, [(i, (i + by) % length) for i in range(length)])  171 us
    dot_general x24, matrix products, contribute(): jnp.einsum('dbp,bkrp->dbkr', shaped, tof[stop_at], preferred_element_type...  38.4 us
    dot_general x24, matrix products, pull(): jnp.einsum('dbkr,bkrp->dbp', picked, tof[stop_at], preferred_element_type...  35.3 us
    unnamed x132, local copies, waits for them, and re-layouts  27.7 us
    all_to_all x3, starting transfers between devices, body(): lax.all_to_all(outgoing, 'sector', split_axis=1, concat_axis=1, tiled=True)  22 us
    gather x24, local copies, waits for them, and re-layouts, pull(): dual_half.reshape(depth_rows, time_blocks, width)[:, tof_rows[stop_at]]  14.6 us
    all_to_all x3, starting transfers between devices, body(): lax.all_to_all(coeffs.astype(jnp.bfloat16), 'sector', split_axis=1, conca...  14.1 us
  transfers between devices with their start and end apart: 60, of which 44 were waited for; matrix products, arithmetic and copies ran while one was open for 23% of the time, Pallas kernels for 0%

commit v1 on v0

--- a/solution.py
+++ b/solution.py
@@ -92,9 +92,12 @@
         forward_data = summed.reshape(depth_rows, time_blocks * width)
         data_dual = (data_dual + dual_step * (forward_data - measured)) / (1.0 + dual_step)
         outgoing = xbar.reshape(depth_rows, sectors, band)[:, inverse, :]
-        tiles = lax.all_to_all(outgoing, "sector", split_axis=1, concat_axis=1, tiled=True).reshape(
-            depth_rows, pixels
-        )
+        tiles = jnp.concatenate(
+            lax.all_to_all(
+                jnp.stack(jnp.split(outgoing, lax.axis_size("sector"), axis=1)), "sector", 0, 0
+            ),
+            axis=1,
+        ).reshape(depth_rows, pixels)
         wavelet_dual = jnp.clip(
             wavelet_dual + dual_step * haar_tiles(tiles), -wave_limit, wave_limit
         )

time: 666 us -> 669 us (level)
    unnamed x132 -> x318, local copies, waits for them, and re-layouts: 27.7 us -> 25.8 us
  transfers between devices with their start and end apart: 60 -> 60, of which waited for: 44 -> 44; matrix products, arithmetic and copies ran while one was open for 23% -> 22% of each run, Pallas kernels for 0% -> 0%
where the time goes in v1:
time: 669 us; the launch traced here: 657 us
  waiting for transfers between devices  272 us (41%)
  starting transfers between devices  220 us (33%)
  matrix products  75.3 us (11%)
  local copies, waits for them, and re-layouts  67.4 us (10%)
  other arithmetic  18.5 us (3%)
    ppermute x48, waiting for transfers between devices, shifted(): lax.ppermute(shard, axis, [(i, (i + by) % length) for i in range(length)])  272 us
    ppermute x48, starting transfers between devices, shifted(): lax.ppermute(shard, axis, [(i, (i + by) % length) for i in range(length)])  166 us
    dot_general x24, matrix products, contribute(): jnp.einsum('dbp,bkrp->dbkr', shaped, tof[stop_at], preferred_element_type...  38.4 us
    dot_general x24, matrix products, pull(): jnp.einsum('dbkr,bkrp->dbp', picked, tof[stop_at], preferred_element_type...  35.3 us
    all_to_all x3, starting transfers between devices, body(): lax.all_to_all(jnp.stack(jnp.split(outgoing, lax.axis_size('sector'), axi...  27.3 us
    unnamed x318, local copies, waits for them, and re-layouts  25.8 us
    gather x24, local copies, waits for them, and re-layouts, pull(): dual_half.reshape(depth_rows, time_blocks, width)[:, tof_rows[stop_at]]  14.6 us
    all_to_all x3, starting transfers between devices, body(): lax.all_to_all(coeffs.astype(jnp.bfloat16), 'sector', split_axis=1, conca...  14.1 us
  transfers between devices with their start and end apart: 60, of which 44 were waited for; matrix products, arithmetic and copies ran while one was open for 22% of the time, Pallas kernels for 0%

profile of v1, /device:TPU:8, one launch (start us, length us, event | category | flops | bytes accessed | tf_op | source)
XLA Modules:
  0.0 657.0 jit_solution(4501457696674054561)
XLA Ops:
  6.9 13.7 %all-to-all-start = ((f32[64,1,512]{2,1,0:T(1,128)}), f32[64,1,512]{2,1,0:T(1,128)S(1)}, u32[]{:S(2)}, u32[]{:S(2)}) async-start(f32[64,1,512]{2,1,0:T(1,128)} %reshape.954), calls=%async_computation | async-start | bytes 262144 | tf_op jit(solution)/shard_map/all_to_all | solution.py:96
  20.6 5.6 collective-permute-start
  46.4 8.1 %collective-permute-start.2 = (bf16[16,2048]{1,0:T(8,128)(2,1)S(1)}, bf16[16,2048]{1,0:T(8,128)(2,1)}, u32[]{:S(2)}, u32[]{:S(2)}) collective-permute-start(bf16[16,2048]{1,0:T(8,128)(2,1)S(1)} %collective-permute-done.1), channel_id=1, source_target_pairs={{0,252},{4,0},{8,4},{12,8},{16,12},{20,16},{24,20},{28,24},{32,28}... | collective-permute-start | bytes 196616 | tf_op jit(solution)/shard_map/ppermute | solution.py:15
  58.9 8.2 %collective-permute-start.3 = (bf16[16,2048]{1,0:T(8,128)(2,1)}, bf16[16,2048]{1,0:T(8,128)(2,1)}, u32[]{:S(2)}, u32[]{:S(2)}) collective-permute-start(bf16[16,2048]{1,0:T(8,128)(2,1)} %collective-permute-done.2), channel_id=1, source_target_pairs={{0,252},{4,0},{8,4},{12,8},{16,12},{20,16},{24,20},{28,24},{32,28}... | collective-permute-start | bytes 196616 | tf_op jit(solution)/shard_map/ppermute | solution.py:15
  85.4 7.6 %collective-permute-start.4 = (bf16[16,2048]{1,0:T(8,128)(2,1)}, bf16[16,2048]{1,0:T(8,128)(2,1)S(1)}, u32[]{:S(2)}, u32[]{:S(2)}) collective-permute-start(bf16[16,2048]{1,0:T(8,128)(2,1)} %collective-permute-done.3), channel_id=1, source_target_pairs={{0,252},{4,0},{8,4},{12,8},{16,12},{20,16},{24,20},{28,24},{32,28}... | collective-permute-start | bytes 196616 | tf_op jit(solution)/shard_map/ppermute | solution.py:15
  96.9 8.2 %collective-permute-start.5 = (bf16[16,2048]{1,0:T(8,128)(2,1)S(1)}, bf16[16,2048]{1,0:T(8,128)(2,1)S(1)}, u32[]{:S(2)}, u32[]{:S(2)}) collective-permute-start(bf16[16,2048]{1,0:T(8,128)(2,1)S(1)} %collective-permute-done.4), channel_id=1, source_target_pairs={{0,252},{4,0},{8,4},{12,8},{16,12},{20,16},{24,20},{28,24},{32,28}... | collective-permute-start | bytes 196616 | tf_op jit(solution)/shard_map/ppermute | solution.py:15
  108.6 8.1 %collective-permute-start.6 = (bf16[16,2048]{1,0:T(8,128)(2,1)S(1)}, bf16[16,2048]{1,0:T(8,128)(2,1)S(1)}, u32[]{:S(2)}, u32[]{:S(2)}) collective-permute-start(bf16[16,2048]{1,0:T(8,128)(2,1)S(1)} %collective-permute-done.5), channel_id=1, source_target_pairs={{0,252},{4,0},{8,4},{12,8},{16,12},{20,16},{24,20},{28,24},{32,28}... | collective-permute-start | bytes 196616 | tf_op jit(solution)/shard_map/ppermute | solution.py:15
  120.3 8.1 %collective-permute-start.7 = (bf16[16,2048]{1,0:T(8,128)(2,1)S(1)}, bf16[16,2048]{1,0:T(8,128)(2,1)S(1)}, u32[]{:S(2)}, u32[]{:S(2)}) collective-permute-start(bf16[16,2048]{1,0:T(8,128)(2,1)S(1)} %collective-permute-done.6), channel_id=1, source_target_pairs={{0,252},{4,0},{8,4},{12,8},{16,12},{20,16},{24,20},{28,24},{32,28}... | collective-permute-start | bytes 196616 | tf_op jit(solution)/shard_map/ppermute | solution.py:15
  140.9 5.7 collective-permute-done.8
  148.1 10.3 %collective-permute-done.9 = f32[16,2048]{1,0:T(8,128)S(1)} collective-permute-done((f32[16,2048]{1,0:T(8,128)S(1)}, f32[16,2048]{1,0:T(8,128)S(1)}, u32[]{:S(2)}, u32[]{:S(2)}) %collective-permute-start.9) | collective-permute-done | bytes 131104 | tf_op jit(solution)/shard_map/ppermute | solution.py:15
  160.0 9.5 %collective-permute-done.10 = f32[16,2048]{1,0:T(8,128)S(1)} collective-permute-done((f32[16,2048]{1,0:T(8,128)S(1)}, f32[16,2048]{1,0:T(8,128)S(1)}, u32[]{:S(2)}, u32[]{:S(2)}) %collective-permute-start.10) | collective-permute-done | bytes 131104 | tf_op jit(solution)/shard_map/ppermute | solution.py:15
  171.0 9.2 %collective-permute-done.11 = f32[16,2048]{1,0:T(8,128)S(1)} collective-permute-done((f32[16,2048]{1,0:T(8,128)S(1)}, f32[16,2048]{1,0:T(8,128)S(1)}, u32[]{:S(2)}, u32[]{:S(2)}) %collective-permute-start.11) | collective-permute-done | bytes 131104 | tf_op jit(solution)/shard_map/ppermute | solution.py:15
  181.8 9.2 %collective-permute-done.12 = f32[16,2048]{1,0:T(8,128)S(1)} collective-permute-done((f32[16,2048]{1,0:T(8,128)S(1)}, f32[16,2048]{1,0:T(8,128)S(1)}, u32[]{:S(2)}, u32[]{:S(2)}) %collective-permute-start.12) | collective-permute-done | bytes 131104 | tf_op jit(solution)/shard_map/ppermute | solution.py:15
  192.6 9.2 %collective-permute-done.13 = f32[16,2048]{1,0:T(8,128)S(1)} collective-permute-done((f32[16,2048]{1,0:T(8,128)S(1)}, f32[16,2048]{1,0:T(8,128)S(1)}, u32[]{:S(2)}, u32[]{:S(2)}) %collective-permute-start.13) | collective-permute-done | bytes 131104 | tf_op jit(solution)/shard_map/ppermute | solution.py:15
  203.4 9.2 %collective-permute-done.14 = f32[16,2048]{1,0:T(8,128)S(1)} collective-permute-done((f32[16,2048]{1,0:T(8,128)S(1)}, f32[16,2048]{1,0:T(8,128)S(1)}, u32[]{:S(2)}, u32[]{:S(2)}) %collective-permute-start.14) | collective-permute-done | bytes 131104 | tf_op jit(solution)/shard_map/ppermute | solution.py:15
  214.2 7.6 %collective-permute-done.15 = f32[16,2048]{1,0:T(8,128)S(1)} collective-permute-done((f32[16,2048]{1,0:T(8,128)S(1)}, f32[16,2048]{1,0:T(8,128)S(1)}, u32[]{:S(2)}, u32[]{:S(2)}) %collective-permute-start.15) | collective-permute-done | bytes 131104 | tf_op jit(solution)/shard_map/ppermute | solution.py:15
  227.5 6.8 %all-to-all-start.2 = ((f32[64,1,512]{2,1,0:T(1,128)}), f32[64,1,512]{2,1,0:T(1,128)S(1)}, u32[]{:S(2)}, u32[]{:S(2)}) async-start(f32[64,1,512]{2,1,0:T(1,128)} %reshape.958), calls=%async_computation.2 | async-start | bytes 262144 | tf_op jit(solution)/shard_map/all_to_all | solution.py:96
  242.4 8.3 %collective-permute-done.18 = bf16[16,2048]{1,0:T(8,128)(2,1)S(1)} collective-permute-done((bf16[16,2048]{1,0:T(8,128)(2,1)S(1)}, bf16[16,2048]{1,0:T(8,128)(2,1)S(1)}, u32[]{:S(2)}, u32[]{:S(2)}) %collective-permute-start.18) | collective-permute-done | bytes 65568 | tf_op jit(solution)/shard_map/ppermute | solution.py:15
  258.3 6.1 collective-permute-start.20
  268.7 8.2 %collective-permute-start.21 = (bf16[16,2048]{1,0:T(8,128)(2,1)}, bf16[16,2048]{1,0:T(8,128)(2,1)}, u32[]{:S(2)}, u32[]{:S(2)}) collective-permute-start(bf16[16,2048]{1,0:T(8,128)(2,1)} %collective-permute-done.20), channel_id=1, source_target_pairs={{0,252},{4,0},{8,4},{12,8},{16,12},{20,16},{24,20},{28,24},{32,28}... | collective-permute-start | bytes 196616 | tf_op jit(solution)/shard_map/ppermute | solution.py:15
  296.0 7.7 %collective-permute-start.22 = (bf16[16,2048]{1,0:T(8,128)(2,1)}, bf16[16,2048]{1,0:T(8,128)(2,1)S(1)}, u32[]{:S(2)}, u32[]{:S(2)}) collective-permute-start(bf16[16,2048]{1,0:T(8,128)(2,1)} %collective-permute-done.21), channel_id=1, source_target_pairs={{0,252},{4,0},{8,4},{12,8},{16,12},{20,16},{24,20},{28,24},{32,28}... | collective-permute-start | bytes 196616 | tf_op jit(solution)/shard_map/ppermute | solution.py:15
  307.5 8.4 %collective-permute-start.23 = (bf16[16,2048]{1,0:T(8,128)(2,1)S(1)}, bf16[16,2048]{1,0:T(8,128)(2,1)S(1)}, u32[]{:S(2)}, u32[]{:S(2)}) collective-permute-start(bf16[16,2048]{1,0:T(8,128)(2,1)S(1)} %collective-permute-done.22), channel_id=1, source_target_pairs={{0,252},{4,0},{8,4},{12,8},{16,12},{20,16},{24,20},{28,24},{32,28}... | collective-permute-start | bytes 196616 | tf_op jit(solution)/shard_map/ppermute | solution.py:15
  319.4 8.1 %collective-permute-start.24 = (bf16[16,2048]{1,0:T(8,128)(2,1)S(1)}, bf16[16,2048]{1,0:T(8,128)(2,1)S(1)}, u32[]{:S(2)}, u32[]{:S(2)}) collective-permute-start(bf16[16,2048]{1,0:T(8,128)(2,1)S(1)} %collective-permute-done.23), channel_id=1, source_target_pairs={{0,252},{4,0},{8,4},{12,8},{16,12},{20,16},{24,20},{28,24},{32,28}... | collective-permute-start | bytes 196616 | tf_op jit(solution)/shard_map/ppermute | solution.py:15
  331.1 8.1 %collective-permute-start.25 = (bf16[16,2048]{1,0:T(8,128)(2,1)S(1)}, bf16[16,2048]{1,0:T(8,128)(2,1)S(1)}, u32[]{:S(2)}, u32[]{:S(2)}) collective-permute-start(bf16[16,2048]{1,0:T(8,128)(2,1)S(1)} %collective-permute-done.24), channel_id=1, source_target_pairs={{0,252},{4,0},{8,4},{12,8},{16,12},{20,16},{24,20},{28,24},{32,28}... | collective-permute-start | bytes 196616 | tf_op jit(solution)/shard_map/ppermute | solution.py:15
  352.4 10.3 %collective-permute-done.26 = f32[16,2048]{1,0:T(8,128)S(1)} collective-permute-done((f32[16,2048]{1,0:T(8,128)S(1)}, f32[16,2048]{1,0:T(8,128)S(1)}, u32[]{:S(2)}, u32[]{:S(2)}) %collective-permute-start.26) | collective-permute-done | bytes 131104 | tf_op jit(solution)/shard_map/ppermute | solution.py:15
  364.3 10.1 %collective-permute-done.27 = f32[16,2048]{1,0:T(8,128)S(1)} collective-permute-done((f32[16,2048]{1,0:T(8,128)S(1)}, f32[16,2048]{1,0:T(8,128)S(1)}, u32[]{:S(2)}, u32[]{:S(2)}) %collective-permute-start.27) | collective-permute-done | bytes 131104 | tf_op jit(solution)/shard_map/ppermute | solution.py:15
  376.0 9.4 %collective-permute-done.28 = f32[16,2048]{1,0:T(8,128)S(1)} collective-permute-done((f32[16,2048]{1,0:T(8,128)S(1)}, f32[16,2048]{1,0:T(8,128)S(1)}, u32[]{:S(2)}, u32[]{:S(2)}) %collective-permute-start.28) | collective-permute-done | bytes 131104 | tf_op jit(solution)/shard_map/ppermute | solution.py:15
  387.0 9.2 %collective-permute-done.29 = f32[16,2048]{1,0:T(8,128)S(1)} collective-permute-done((f32[16,2048]{1,0:T(8,128)S(1)}, f32[16,2048]{1,0:T(8,128)S(1)}, u32[]{:S(2)}, u32[]{:S(2)}) %collective-permute-start.29) | collective-permute-done | bytes 131104 | tf_op jit(solution)/shard_map/ppermute | solution.py:15
  397.7 9.2 %collective-permute-done.30 = f32[16,2048]{1,0:T(8,128)S(1)} collective-permute-done((f32[16,2048]{1,0:T(8,128)S(1)}, f32[16,2048]{1,0:T(8,128)S(1)}, u32[]{:S(2)}, u32[]{:S(2)}) %collective-permute-start.30) | collective-permute-done | bytes 131104 | tf_op jit(solution)/shard_map/ppermute | solution.py:15
  408.5 9.2 %collective-permute-done.31 = f32[16,2048]{1,0:T(8,128)S(1)} collective-permute-done((f32[16,2048]{1,0:T(8,128)S(1)}, f32[16,2048]{1,0:T(8,128)S(1)}, u32[]{:S(2)}, u32[]{:S(2)}) %collective-permute-start.31) | collective-permute-done | bytes 131104 | tf_op jit(solution)/shard_map/ppermute | solution.py:15
  419.3 9.2 %collective-permute-done.32 = f32[16,2048]{1,0:T(8,128)S(1)} collective-permute-done((f32[16,2048]{1,0:T(8,128)S(1)}, f32[16,2048]{1,0:T(8,128)S(1)}, u32[]{:S(2)}, u32[]{:S(2)}) %collective-permute-start.32) | collective-permute-done | bytes 131104 | tf_op jit(solution)/shard_map/ppermute | solution.py:15
  430.1 7.6 %collective-permute-done.33 = f32[16,2048]{1,0:T(8,128)S(1)} collective-permute-done((f32[16,2048]{1,0:T(8,128)S(1)}, f32[16,2048]{1,0:T(8,128)S(1)}, u32[]{:S(2)}, u32[]{:S(2)}) %collective-permute-start.33) | collective-permute-done | bytes 131104 | tf_op jit(solution)/shard_map/ppermute | solution.py:15
  443.9 6.8 %all-to-all-start.4 = ((f32[64,1,512]{2,1,0:T(1,128)}), f32[64,1,512]{2,1,0:T(1,128)S(1)}, u32[]{:S(2)}, u32[]{:S(2)}) async-start(f32[64,1,512]{2,1,0:T(1,128)} %reshape.962), calls=%async_computation.4 | async-start | bytes 262144 | tf_op jit(solution)/shard_map/all_to_all | solution.py:96
  458.9 8.3 %collective-permute-done.36 = bf16[16,2048]{1,0:T(8,128)(2,1)S(1)} collective-permute-done((bf16[16,2048]{1,0:T(8,128)(2,1)S(1)}, bf16[16,2048]{1,0:T(8,128)(2,1)S(1)}, u32[]{:S(2)}, u32[]{:S(2)}) %collective-permute-start.36) | collective-permute-done | bytes 65568 | tf_op jit(solution)/shard_map/ppermute | solution.py:15
  474.8 6.1 collective-permute-start.38
  484.4 8.1 %collective-permute-start.39 = (bf16[16,2048]{1,0:T(8,128)(2,1)S(1)}, bf16[16,2048]{1,0:T(8,128)(2,1)S(1)}, u32[]{:S(2)}, u32[]{:S(2)}) collective-permute-start(bf16[16,2048]{1,0:T(8,128)(2,1)S(1)} %collective-permute-done.38), channel_id=1, source_target_pairs={{0,252},{4,0},{8,4},{12,8},{16,12},{20,16},{24,20},{28,24},{32,28}... | collective-permute-start | bytes 196616 | tf_op jit(solution)/shard_map/ppermute | solution.py:15
  514.0 7.9 %collective-permute-start.40 = (bf16[16,2048]{1,0:T(8,128)(2,1)S(1)}, bf16[16,2048]{1,0:T(8,128)(2,1)S(1)}, u32[]{:S(2)}, u32[]{:S(2)}) collective-permute-start(bf16[16,2048]{1,0:T(8,128)(2,1)S(1)} %collective-permute-done.39), channel_id=1, source_target_pairs={{0,252},{4,0},{8,4},{12,8},{16,12},{20,16},{24,20},{28,24},{32,28}... | collective-permute-start | bytes 196616 | tf_op jit(solution)/shard_map/ppermute | solution.py:15
  525.4 8.1 %collective-permute-start.41 = (bf16[16,2048]{1,0:T(8,128)(2,1)S(1)}, bf16[16,2048]{1,0:T(8,128)(2,1)S(1)}, u32[]{:S(2)}, u32[]{:S(2)}) collective-permute-start(bf16[16,2048]{1,0:T(8,128)(2,1)S(1)} %collective-permute-done.40), channel_id=1, source_target_pairs={{0,252},{4,0},{8,4},{12,8},{16,12},{20,16},{24,20},{28,24},{32,28}... | collective-permute-start | bytes 196616 | tf_op jit(solution)/shard_map/ppermute | solution.py:15
  537.0 8.1 %collective-permute-start.42 = (bf16[16,2048]{1,0:T(8,128)(2,1)S(1)}, bf16[16,2048]{1,0:T(8,128)(2,1)S(1)}, u32[]{:S(2)}, u32[]{:S(2)}) collective-permute-start(bf16[16,2048]{1,0:T(8,128)(2,1)S(1)} %collective-permute-done.41), channel_id=1, source_target_pairs={{0,252},{4,0},{8,4},{12,8},{16,12},{20,16},{24,20},{28,24},{32,28}... | collective-permute-start | bytes 196616 | tf_op jit(solution)/shard_map/ppermute | solution.py:15
  548.7 8.1 %collective-permute-start.43 = (bf16[16,2048]{1,0:T(8,128)(2,1)S(1)}, bf16[16,2048]{1,0:T(8,128)(2,1)S(1)}, u32[]{:S(2)}, u32[]{:S(2)}) collective-permute-start(bf16[16,2048]{1,0:T(8,128)(2,1)S(1)} %collective-permute-done.42), channel_id=1, source_target_pairs={{0,252},{4,0},{8,4},{12,8},{16,12},{20,16},{24,20},{28,24},{32,28}... | collective-permute-start | bytes 196616 | tf_op jit(solution)/shard_map/ppermute | solution.py:15
  570.2 10.3 %collective-permute-done.44 = f32[16,2048]{1,0:T(8,128)S(1)} collective-permute-done((f32[16,2048]{1,0:T(8,128)S(1)}, f32[16,2048]{1,0:T(8,128)S(1)}, u32[]{:S(2)}, u32[]{:S(2)}) %collective-permute-start.44) | collective-permute-done | bytes 131104 | tf_op jit(solution)/shard_map/ppermute | solution.py:15
  582.0 10.1 %collective-permute-done.45 = f32[16,2048]{1,0:T(8,128)S(1)} collective-permute-done((f32[16,2048]{1,0:T(8,128)S(1)}, f32[16,2048]{1,0:T(8,128)S(1)}, u32[]{:S(2)}, u32[]{:S(2)}) %collective-permute-start.45) | collective-permute-done | bytes 131104 | tf_op jit(solution)/shard_map/ppermute | solution.py:15
  593.8 9.4 %collective-permute-done.46 = f32[16,2048]{1,0:T(8,128)S(1)} collective-permute-done((f32[16,2048]{1,0:T(8,128)S(1)}, f32[16,2048]{1,0:T(8,128)S(1)}, u32[]{:S(2)}, u32[]{:S(2)}) %collective-permute-start.46) | collective-permute-done | bytes 131104 | tf_op jit(solution)/shard_map/ppermute | solution.py:15
  604.7 9.2 %collective-permute-done.47 = f32[16,2048]{1,0:T(8,128)S(1)} collective-permute-done((f32[16,2048]{1,0:T(8,128)S(1)}, f32[16,2048]{1,0:T(8,128)S(1)}, u32[]{:S(2)}, u32[]{:S(2)}) %collective-permute-start.47) | collective-permute-done | bytes 131104 | tf_op jit(solution)/shard_map/ppermute | solution.py:15
  615.5 9.2 %collective-permute-done.48 = f32[16,2048]{1,0:T(8,128)S(1)} collective-permute-done((f32[16,2048]{1,0:T(8,128)S(1)}, f32[16,2048]{1,0:T(8,128)S(1)}, u32[]{:S(2)}, u32[]{:S(2)}) %collective-permute-start.48) | collective-permute-done | bytes 131104 | tf_op jit(solution)/shard_map/ppermute | solution.py:15
  626.3 9.2 %collective-permute-done.49 = f32[16,2048]{1,0:T(8,128)S(1)} collective-permute-done((f32[16,2048]{1,0:T(8,128)S(1)}, f32[16,2048]{1,0:T(8,128)S(1)}, u32[]{:S(2)}, u32[]{:S(2)}) %collective-permute-start.49) | collective-permute-done | bytes 131104 | tf_op jit(solution)/shard_map/ppermute | solution.py:15
  637.1 9.2 %collective-permute-done.50 = f32[16,2048]{1,0:T(8,128)S(1)} collective-permute-done((f32[16,2048]{1,0:T(8,128)S(1)}, f32[16,2048]{1,0:T(8,128)S(1)}, u32[]{:S(2)}, u32[]{:S(2)}) %collective-permute-start.50) | collective-permute-done | bytes 131104 | tf_op jit(solution)/shard_map/ppermute | solution.py:15
  647.6 7.6 %collective-permute-done.51 = f32[16,2048]{1,0:T(8,128)S(1)} collective-permute-done((f32[16,2048]{1,0:T(8,128)S(1)}, f32[16,2048]{1,0:T(8,128)S(1)}, u32[]{:S(2)}, u32[]{:S(2)}) %collective-permute-start.51) | collective-permute-done | bytes 131104 | tf_op jit(solution)/shard_map/ppermute | solution.py:15
  (613 shorter events, 243.6 us)
Async XLA Ops:
  6.9 60.3 %all-to-all-start = ((f32[64,1,512]{2,1,0:T(1,128)}), f32[64,1,512]{2,1,0:T(1,128)S(1)}, u32[]{:S(2)}, u32[]{:S(2)}) async-start(f32[64,1,512]{2,1,0:T(1,128)} %reshape.954), calls=%async_computation | async-start | bytes 262144 | tf_op jit(solution)/shard_map/all_to_all | solution.py:96
  20.6 15.6 %collective-permute-start = (bf16[16,2048]{1,0:T(8,128)(2,1)S(1)}, bf16[16,2048]{1,0:T(8,128)(2,1)S(1)}, u32[]{:S(2)}, u32[]{:S(2)}) collective-permute-start(bf16[16,2048]{1,0:T(8,128)(2,1)S(1)} %convert_element_type.67), channel_id=1, source_target_pairs={{0,16},{4,20},{8,24},{12,28},{16,32},{20,36},{24,40},{28,44},{32,4... | collective-permute-start | bytes 196616 | tf_op jit(solution)/shard_map/ppermute | solution.py:15
  33.7 180.4 %collective-permute-start.17 = (f32[1,2048]{1,0:T(1,128)}, f32[1,2048]{1,0:T(1,128)}, u32[]{:S(2)}, u32[]{:S(2)}) collective-permute-start(f32[1,2048]{1,0:T(1,128)} %slice.405), channel_id=1, source_target_pairs={{0,1},{1,2},{2,3},{4,5},{5,6},{6,7},{8,9},{9,10},{10,11},{12,13},{... | collective-permute-start | bytes 24584 | tf_op jit(solution)/shard_map/ppermute | solution.py:21
  46.4 10.0 %collective-permute-start.2 = (bf16[16,2048]{1,0:T(8,128)(2,1)S(1)}, bf16[16,2048]{1,0:T(8,128)(2,1)}, u32[]{:S(2)}, u32[]{:S(2)}) collective-permute-start(bf16[16,2048]{1,0:T(8,128)(2,1)S(1)} %collective-permute-done.1), channel_id=1, source_target_pairs={{0,252},{4,0},{8,4},{12,8},{16,12},{20,16},{24,20},{28,24},{32,28}... | collective-permute-start | bytes 196616 | tf_op jit(solution)/shard_map/ppermute | solution.py:15
  58.9 24.1 %collective-permute-start.3 = (bf16[16,2048]{1,0:T(8,128)(2,1)}, bf16[16,2048]{1,0:T(8,128)(2,1)}, u32[]{:S(2)}, u32[]{:S(2)}) collective-permute-start(bf16[16,2048]{1,0:T(8,128)(2,1)} %collective-permute-done.2), channel_id=1, source_target_pairs={{0,252},{4,0},{8,4},{12,8},{16,12},{20,16},{24,20},{28,24},{32,28}... | collective-permute-start | bytes 196616 | tf_op jit(solution)/shard_map/ppermute | solution.py:15
  78.3 26.8 %all-to-all-start.1 = ((bf16[64,2,256]{2,1,0:T(2,128)(2,1)}), bf16[64,2,256]{2,1,0:T(2,128)(2,1)S(1)}, u32[]{:S(2)}, u32[]{:S(2)}) async-start(bf16[64,2,256]{2,1,0:T(2,128)(2,1)} %reshape.956), calls=%async_computation.1 | async-start | bytes 131072 | tf_op jit(solution)/shard_map/all_to_all | solution.py:115
  96.9 10.1 %collective-permute-start.5 = (bf16[16,2048]{1,0:T(8,128)(2,1)S(1)}, bf16[16,2048]{1,0:T(8,128)(2,1)S(1)}, u32[]{:S(2)}, u32[]{:S(2)}) collective-permute-start(bf16[16,2048]{1,0:T(8,128)(2,1)S(1)} %collective-permute-done.4), channel_id=1, source_target_pairs={{0,252},{4,0},{8,4},{12,8},{16,12},{20,16},{24,20},{28,24},{32,28}... | collective-permute-start | bytes 196616 | tf_op jit(solution)/shard_map/ppermute | solution.py:15
  108.6 10.0 %collective-permute-start.6 = (bf16[16,2048]{1,0:T(8,128)(2,1)S(1)}, bf16[16,2048]{1,0:T(8,128)(2,1)S(1)}, u32[]{:S(2)}, u32[]{:S(2)}) collective-permute-start(bf16[16,2048]{1,0:T(8,128)(2,1)S(1)} %collective-permute-done.5), channel_id=1, source_target_pairs={{0,252},{4,0},{8,4},{12,8},{16,12},{20,16},{24,20},{28,24},{32,28}... | collective-permute-start | bytes 196616 | tf_op jit(solution)/shard_map/ppermute | solution.py:15
  120.3 10.0 %collective-permute-start.7 = (bf16[16,2048]{1,0:T(8,128)(2,1)S(1)}, bf16[16,2048]{1,0:T(8,128)(2,1)S(1)}, u32[]{:S(2)}, u32[]{:S(2)}) collective-permute-start(bf16[16,2048]{1,0:T(8,128)(2,1)S(1)} %collective-permute-done.6), channel_id=1, source_target_pairs={{0,252},{4,0},{8,4},{12,8},{16,12},{20,16},{24,20},{28,24},{32,28}... | collective-permute-start | bytes 196616 | tf_op jit(solution)/shard_map/ppermute | solution.py:15
  134.9 11.7 %collective-permute-start.8 = (f32[16,2048]{1,0:T(8,128)S(1)}, f32[16,2048]{1,0:T(8,128)S(1)}, u32[]{:S(2)}, u32[]{:S(2)}) collective-permute-start(f32[16,2048]{1,0:T(8,128)S(1)} %bitcast.1817), channel_id=1, source_target_pairs={{0,4},{4,8},{8,12},{12,16},{16,20},{20,24},{24,28},{28,32},{32,36}... | collective-permute-start | bytes 393224 | tf_op jit(solution)/shard_map/ppermute | solution.py:15
  146.5 11.9 %collective-permute-start.9 = (f32[16,2048]{1,0:T(8,128)S(1)}, f32[16,2048]{1,0:T(8,128)S(1)}, u32[]{:S(2)}, u32[]{:S(2)}) collective-permute-start(f32[16,2048]{1,0:T(8,128)S(1)} %bitcast_add_fusion.20), channel_id=1, source_target_pairs={{0,4},{4,8},{8,12},{12,16},{16,20},{20,24},{24,28},{28,32},{32,36}... | collective-permute-start | bytes 393224 | tf_op jit(solution)/shard_map/ppermute | solution.py:15
  158.4 11.0 %collective-permute-start.10 = (f32[16,2048]{1,0:T(8,128)S(1)}, f32[16,2048]{1,0:T(8,128)S(1)}, u32[]{:S(2)}, u32[]{:S(2)}) collective-permute-start(f32[16,2048]{1,0:T(8,128)S(1)} %bitcast_add_fusion.19), channel_id=1, source_target_pairs={{0,4},{4,8},{8,12},{12,16},{16,20},{20,24},{24,28},{28,32},{32,36}... | collective-permute-start | bytes 393224 | tf_op jit(solution)/shard_map/ppermute | solution.py:15
  169.5 10.8 %collective-permute-start.11 = (f32[16,2048]{1,0:T(8,128)S(1)}, f32[16,2048]{1,0:T(8,128)S(1)}, u32[]{:S(2)}, u32[]{:S(2)}) collective-permute-start(f32[16,2048]{1,0:T(8,128)S(1)} %bitcast_add_fusion.18), channel_id=1, source_target_pairs={{0,4},{4,8},{8,12},{12,16},{16,20},{20,24},{24,28},{28,32},{32,36}... | collective-permute-start | bytes 393224 | tf_op jit(solution)/shard_map/ppermute | solution.py:15
  180.3 10.8 %collective-permute-start.12 = (f32[16,2048]{1,0:T(8,128)S(1)}, f32[16,2048]{1,0:T(8,128)S(1)}, u32[]{:S(2)}, u32[]{:S(2)}) collective-permute-start(f32[16,2048]{1,0:T(8,128)S(1)} %bitcast_add_fusion.17), channel_id=1, source_target_pairs={{0,4},{4,8},{8,12},{12,16},{16,20},{20,24},{24,28},{28,32},{32,36}... | collective-permute-start | bytes 393224 | tf_op jit(solution)/shard_map/ppermute | solution.py:15
  191.1 10.8 %collective-permute-start.13 = (f32[16,2048]{1,0:T(8,128)S(1)}, f32[16,2048]{1,0:T(8,128)S(1)}, u32[]{:S(2)}, u32[]{:S(2)}) collective-permute-start(f32[16,2048]{1,0:T(8,128)S(1)} %bitcast_add_fusion.16), channel_id=1, source_target_pairs={{0,4},{4,8},{8,12},{12,16},{16,20},{20,24},{24,28},{28,32},{32,36}... | collective-permute-start | bytes 393224 | tf_op jit(solution)/shard_map/ppermute | solution.py:15
  201.8 10.8 %collective-permute-start.14 = (f32[16,2048]{1,0:T(8,128)S(1)}, f32[16,2048]{1,0:T(8,128)S(1)}, u32[]{:S(2)}, u32[]{:S(2)}) collective-permute-start(f32[16,2048]{1,0:T(8,128)S(1)} %bitcast_add_fusion.15), channel_id=1, source_target_pairs={{0,4},{4,8},{8,12},{12,16},{16,20},{20,24},{24,28},{28,32},{32,36}... | collective-permute-start | bytes 393224 | tf_op jit(solution)/shard_map/ppermute | solution.py:15
  224.6 15.2 %collective-permute-start.34 = (f32[1,2048]{1,0:T(1,128)S(1)}, f32[1,2048]{1,0:T(1,128)S(1)}, u32[]{:S(2)}, u32[]{:S(2)}) collective-permute-start(f32[1,2048]{1,0:T(1,128)S(1)} %slice.420), channel_id=1, source_target_pairs={{1,0},{2,1},{3,2},{5,4},{6,5},{7,6},{9,8},{10,9},{11,10},{13,12},{... | collective-permute-start | bytes 24584 | tf_op jit(solution)/shard_map/ppermute | solution.py:21
  227.5 49.6 %all-to-all-start.2 = ((f32[64,1,512]{2,1,0:T(1,128)}), f32[64,1,512]{2,1,0:T(1,128)S(1)}, u32[]{:S(2)}, u32[]{:S(2)}) async-start(f32[64,1,512]{2,1,0:T(1,128)} %reshape.958), calls=%async_computation.2 | async-start | bytes 262144 | tf_op jit(solution)/shard_map/all_to_all | solution.py:96
  234.3 16.5 %collective-permute-start.18 = (bf16[16,2048]{1,0:T(8,128)(2,1)S(1)}, bf16[16,2048]{1,0:T(8,128)(2,1)S(1)}, u32[]{:S(2)}, u32[]{:S(2)}) collective-permute-start(bf16[16,2048]{1,0:T(8,128)(2,1)S(1)} %get-tuple-element.19), channel_id=1, source_target_pairs={{0,16},{4,20},{8,24},{12,28},{16,32},{20,36},{24,40},{28,44},{32,4... | collective-permute-start | bytes 196616 | tf_op jit(solution)/shard_map/ppermute | solution.py:15
  240.5 189.5 %collective-permute-start.35 = (f32[1,2048]{1,0:T(1,128)}, f32[1,2048]{1,0:T(1,128)}, u32[]{:S(2)}, u32[]{:S(2)}) collective-permute-start(f32[1,2048]{1,0:T(1,128)} %slice.421), channel_id=1, source_target_pairs={{0,1},{1,2},{2,3},{4,5},{5,6},{6,7},{8,9},{9,10},{10,11},{12,13},{... | collective-permute-start | bytes 24584 | tf_op jit(solution)/shard_map/ppermute | solution.py:21
  268.7 24.7 %collective-permute-start.21 = (bf16[16,2048]{1,0:T(8,128)(2,1)}, bf16[16,2048]{1,0:T(8,128)(2,1)}, u32[]{:S(2)}, u32[]{:S(2)}) collective-permute-start(bf16[16,2048]{1,0:T(8,128)(2,1)} %collective-permute-done.20), channel_id=1, source_target_pairs={{0,252},{4,0},{8,4},{12,8},{16,12},{20,16},{24,20},{28,24},{32,28}... | collective-permute-start | bytes 196616 | tf_op jit(solution)/shard_map/ppermute | solution.py:15
  288.7 27.3 %all-to-all-start.3 = ((bf16[64,2,256]{2,1,0:T(2,128)(2,1)}), bf16[64,2,256]{2,1,0:T(2,128)(2,1)S(1)}, u32[]{:S(2)}, u32[]{:S(2)}) async-start(bf16[64,2,256]{2,1,0:T(2,128)(2,1)} %reshape.960), calls=%async_computation.3 | async-start | bytes 131072 | tf_op jit(solution)/shard_map/all_to_all | solution.py:115
  307.5 10.3 %collective-permute-start.23 = (bf16[16,2048]{1,0:T(8,128)(2,1)S(1)}, bf16[16,2048]{1,0:T(8,128)(2,1)S(1)}, u32[]{:S(2)}, u32[]{:S(2)}) collective-permute-start(bf16[16,2048]{1,0:T(8,128)(2,1)S(1)} %collective-permute-done.22), channel_id=1, source_target_pairs={{0,252},{4,0},{8,4},{12,8},{16,12},{20,16},{24,20},{28,24},{32,28}... | collective-permute-start | bytes 196616 | tf_op jit(solution)/shard_map/ppermute | solution.py:15
  319.4 10.0 %collective-permute-start.24 = (bf16[16,2048]{1,0:T(8,128)(2,1)S(1)}, bf16[16,2048]{1,0:T(8,128)(2,1)S(1)}, u32[]{:S(2)}, u32[]{:S(2)}) collective-permute-start(bf16[16,2048]{1,0:T(8,128)(2,1)S(1)} %collective-permute-done.23), channel_id=1, source_target_pairs={{0,252},{4,0},{8,4},{12,8},{16,12},{20,16},{24,20},{28,24},{32,28}... | collective-permute-start | bytes 196616 | tf_op jit(solution)/shard_map/ppermute | solution.py:15
  331.1 10.0 %collective-permute-start.25 = (bf16[16,2048]{1,0:T(8,128)(2,1)S(1)}, bf16[16,2048]{1,0:T(8,128)(2,1)S(1)}, u32[]{:S(2)}, u32[]{:S(2)}) collective-permute-start(bf16[16,2048]{1,0:T(8,128)(2,1)S(1)} %collective-permute-done.24), channel_id=1, source_target_pairs={{0,252},{4,0},{8,4},{12,8},{16,12},{20,16},{24,20},{28,24},{32,28}... | collective-permute-start | bytes 196616 | tf_op jit(solution)/shard_map/ppermute | solution.py:15
  350.9 11.8 %collective-permute-start.26 = (f32[16,2048]{1,0:T(8,128)S(1)}, f32[16,2048]{1,0:T(8,128)S(1)}, u32[]{:S(2)}, u32[]{:S(2)}) collective-permute-start(f32[16,2048]{1,0:T(8,128)S(1)} %bitcast.1818), channel_id=1, source_target_pairs={{0,4},{4,8},{8,12},{12,16},{16,20},{20,24},{24,28},{28,32},{32,36}... | collective-permute-start | bytes 393224 | tf_op jit(solution)/shard_map/ppermute | solution.py:15
  362.7 11.7 %collective-permute-start.27 = (f32[16,2048]{1,0:T(8,128)S(1)}, f32[16,2048]{1,0:T(8,128)S(1)}, u32[]{:S(2)}, u32[]{:S(2)}) collective-permute-start(f32[16,2048]{1,0:T(8,128)S(1)} %bitcast_add_fusion.13), channel_id=1, source_target_pairs={{0,4},{4,8},{8,12},{12,16},{16,20},{20,24},{24,28},{28,32},{32,36}... | collective-permute-start | bytes 393224 | tf_op jit(solution)/shard_map/ppermute | solution.py:15
  374.5 10.9 %collective-permute-start.28 = (f32[16,2048]{1,0:T(8,128)S(1)}, f32[16,2048]{1,0:T(8,128)S(1)}, u32[]{:S(2)}, u32[]{:S(2)}) collective-permute-start(f32[16,2048]{1,0:T(8,128)S(1)} %bitcast_add_fusion.12), channel_id=1, source_target_pairs={{0,4},{4,8},{8,12},{12,16},{16,20},{20,24},{24,28},{28,32},{32,36}... | collective-permute-start | bytes 393224 | tf_op jit(solution)/shard_map/ppermute | solution.py:15
  385.4 10.8 %collective-permute-start.29 = (f32[16,2048]{1,0:T(8,128)S(1)}, f32[16,2048]{1,0:T(8,128)S(1)}, u32[]{:S(2)}, u32[]{:S(2)}) collective-permute-start(f32[16,2048]{1,0:T(8,128)S(1)} %bitcast_add_fusion.11), channel_id=1, source_target_pairs={{0,4},{4,8},{8,12},{12,16},{16,20},{20,24},{24,28},{28,32},{32,36}... | collective-permute-start | bytes 393224 | tf_op jit(solution)/shard_map/ppermute | solution.py:15
  396.2 10.8 %collective-permute-start.30 = (f32[16,2048]{1,0:T(8,128)S(1)}, f32[16,2048]{1,0:T(8,128)S(1)}, u32[]{:S(2)}, u32[]{:S(2)}) collective-permute-start(f32[16,2048]{1,0:T(8,128)S(1)} %bitcast_add_fusion.10), channel_id=1, source_target_pairs={{0,4},{4,8},{8,12},{12,16},{16,20},{20,24},{24,28},{28,32},{32,36}... | collective-permute-start | bytes 393224 | tf_op jit(solution)/shard_map/ppermute | solution.py:15
  407.0 10.8 %collective-permute-start.31 = (f32[16,2048]{1,0:T(8,128)S(1)}, f32[16,2048]{1,0:T(8,128)S(1)}, u32[]{:S(2)}, u32[]{:S(2)}) collective-permute-start(f32[16,2048]{1,0:T(8,128)S(1)} %bitcast_add_fusion.9), channel_id=1, source_target_pairs={{0,4},{4,8},{8,12},{12,16},{16,20},{20,24},{24,28},{28,32},{32,36}... | collective-permute-start | bytes 393224 | tf_op jit(solution)/shard_map/ppermute | solution.py:15
  417.8 10.8 %collective-permute-start.32 = (f32[16,2048]{1,0:T(8,128)S(1)}, f32[16,2048]{1,0:T(8,128)S(1)}, u32[]{:S(2)}, u32[]{:S(2)}) collective-permute-start(f32[16,2048]{1,0:T(8,128)S(1)} %bitcast_add_fusion.8), channel_id=1, source_target_pairs={{0,4},{4,8},{8,12},{12,16},{16,20},{20,24},{24,28},{28,32},{32,36}... | collective-permute-start | bytes 393224 | tf_op jit(solution)/shard_map/ppermute | solution.py:15
  441.0 15.2 %collective-permute-start.52 = (f32[1,2048]{1,0:T(1,128)S(1)}, f32[1,2048]{1,0:T(1,128)S(1)}, u32[]{:S(2)}, u32[]{:S(2)}) collective-permute-start(f32[1,2048]{1,0:T(1,128)S(1)} %slice.436), channel_id=1, source_target_pairs={{1,0},{2,1},{3,2},{5,4},{6,5},{7,6},{9,8},{10,9},{11,10},{13,12},{... | collective-permute-start | bytes 24584 | tf_op jit(solution)/shard_map/ppermute | solution.py:21
  443.9 48.6 %all-to-all-start.4 = ((f32[64,1,512]{2,1,0:T(1,128)}), f32[64,1,512]{2,1,0:T(1,128)S(1)}, u32[]{:S(2)}, u32[]{:S(2)}) async-start(f32[64,1,512]{2,1,0:T(1,128)} %reshape.962), calls=%async_computation.4 | async-start | bytes 262144 | tf_op jit(solution)/shard_map/all_to_all | solution.py:96
  450.7 16.5 %collective-permute-start.36 = (bf16[16,2048]{1,0:T(8,128)(2,1)S(1)}, bf16[16,2048]{1,0:T(8,128)(2,1)S(1)}, u32[]{:S(2)}, u32[]{:S(2)}) collective-permute-start(bf16[16,2048]{1,0:T(8,128)(2,1)S(1)} %get-tuple-element.16), channel_id=1, source_target_pairs={{0,16},{4,20},{8,24},{12,28},{16,32},{20,36},{24,40},{28,44},{32,4... | collective-permute-start | bytes 196616 | tf_op jit(solution)/shard_map/ppermute | solution.py:15
  457.0 190.6 %collective-permute-start.53 = (f32[1,2048]{1,0:T(1,128)}, f32[1,2048]{1,0:T(1,128)}, u32[]{:S(2)}, u32[]{:S(2)}) collective-permute-start(f32[1,2048]{1,0:T(1,128)} %slice.437), channel_id=1, source_target_pairs={{0,1},{1,2},{2,3},{4,5},{5,6},{6,7},{8,9},{9,10},{10,11},{12,13},{... | collective-permute-start | bytes 24584 | tf_op jit(solution)/shard_map/ppermute | solution.py:21
  484.4 28.0 %collective-permute-start.39 = (bf16[16,2048]{1,0:T(8,128)(2,1)S(1)}, bf16[16,2048]{1,0:T(8,128)(2,1)S(1)}, u32[]{:S(2)}, u32[]{:S(2)}) collective-permute-start(bf16[16,2048]{1,0:T(8,128)(2,1)S(1)} %collective-permute-done.38), channel_id=1, source_target_pairs={{0,252},{4,0},{8,4},{12,8},{16,12},{20,16},{24,20},{28,24},{32,28}... | collective-permute-start | bytes 196616 | tf_op jit(solution)/shard_map/ppermute | solution.py:15
  505.4 28.2 %all-to-all-start.5 = ((bf16[64,2,256]{2,1,0:T(2,128)(2,1)}), bf16[64,2,256]{2,1,0:T(2,128)(2,1)S(1)}, u32[]{:S(2)}, u32[]{:S(2)}) async-start(bf16[64,2,256]{2,1,0:T(2,128)(2,1)} %reshape.964), calls=%async_computation.5 | async-start | bytes 131072 | tf_op jit(solution)/shard_map/all_to_all | solution.py:115
  525.4 10.0 %collective-permute-start.41 = (bf16[16,2048]{1,0:T(8,128)(2,1)S(1)}, bf16[16,2048]{1,0:T(8,128)(2,1)S(1)}, u32[]{:S(2)}, u32[]{:S(2)}) collective-permute-start(bf16[16,2048]{1,0:T(8,128)(2,1)S(1)} %collective-permute-done.40), channel_id=1, source_target_pairs={{0,252},{4,0},{8,4},{12,8},{16,12},{20,16},{24,20},{28,24},{32,28}... | collective-permute-start | bytes 196616 | tf_op jit(solution)/shard_map/ppermute | solution.py:15
  537.0 10.0 %collective-permute-start.42 = (bf16[16,2048]{1,0:T(8,128)(2,1)S(1)}, bf16[16,2048]{1,0:T(8,128)(2,1)S(1)}, u32[]{:S(2)}, u32[]{:S(2)}) collective-permute-start(bf16[16,2048]{1,0:T(8,128)(2,1)S(1)} %collective-permute-done.41), channel_id=1, source_target_pairs={{0,252},{4,0},{8,4},{12,8},{16,12},{20,16},{24,20},{28,24},{32,28}... | collective-permute-start | bytes 196616 | tf_op jit(solution)/shard_map/ppermute | solution.py:15
  548.7 10.0 %collective-permute-start.43 = (bf16[16,2048]{1,0:T(8,128)(2,1)S(1)}, bf16[16,2048]{1,0:T(8,128)(2,1)S(1)}, u32[]{:S(2)}, u32[]{:S(2)}) collective-permute-start(bf16[16,2048]{1,0:T(8,128)(2,1)S(1)} %collective-permute-done.42), channel_id=1, source_target_pairs={{0,252},{4,0},{8,4},{12,8},{16,12},{20,16},{24,20},{28,24},{32,28}... | collective-permute-start | bytes 196616 | tf_op jit(solution)/shard_map/ppermute | solution.py:15
  568.6 11.8 %collective-permute-start.44 = (f32[16,2048]{1,0:T(8,128)S(1)}, f32[16,2048]{1,0:T(8,128)S(1)}, u32[]{:S(2)}, u32[]{:S(2)}) collective-permute-start(f32[16,2048]{1,0:T(8,128)S(1)} %bitcast.1819), channel_id=1, source_target_pairs={{0,4},{4,8},{8,12},{12,16},{16,20},{20,24},{24,28},{28,32},{32,36}... | collective-permute-start | bytes 393224 | tf_op jit(solution)/shard_map/ppermute | solution.py:15
  580.5 11.7 %collective-permute-start.45 = (f32[16,2048]{1,0:T(8,128)S(1)}, f32[16,2048]{1,0:T(8,128)S(1)}, u32[]{:S(2)}, u32[]{:S(2)}) collective-permute-start(f32[16,2048]{1,0:T(8,128)S(1)} %bitcast_add_fusion.6), channel_id=1, source_target_pairs={{0,4},{4,8},{8,12},{12,16},{16,20},{20,24},{24,28},{28,32},{32,36}... | collective-permute-start | bytes 393224 | tf_op jit(solution)/shard_map/ppermute | solution.py:15
  592.2 10.9 %collective-permute-start.46 = (f32[16,2048]{1,0:T(8,128)S(1)}, f32[16,2048]{1,0:T(8,128)S(1)}, u32[]{:S(2)}, u32[]{:S(2)}) collective-permute-start(f32[16,2048]{1,0:T(8,128)S(1)} %bitcast_add_fusion.5), channel_id=1, source_target_pairs={{0,4},{4,8},{8,12},{12,16},{16,20},{20,24},{24,28},{28,32},{32,36}... | collective-permute-start | bytes 393224 | tf_op jit(solution)/shard_map/ppermute | solution.py:15
  603.1 10.8 %collective-permute-start.47 = (f32[16,2048]{1,0:T(8,128)S(1)}, f32[16,2048]{1,0:T(8,128)S(1)}, u32[]{:S(2)}, u32[]{:S(2)}) collective-permute-start(f32[16,2048]{1,0:T(8,128)S(1)} %bitcast_add_fusion.4), channel_id=1, source_target_pairs={{0,4},{4,8},{8,12},{12,16},{16,20},{20,24},{24,28},{28,32},{32,36}... | collective-permute-start | bytes 393224 | tf_op jit(solution)/shard_map/ppermute | solution.py:15
  613.9 10.8 %collective-permute-start.48 = (f32[16,2048]{1,0:T(8,128)S(1)}, f32[16,2048]{1,0:T(8,128)S(1)}, u32[]{:S(2)}, u32[]{:S(2)}) collective-permute-start(f32[16,2048]{1,0:T(8,128)S(1)} %bitcast_add_fusion.3), channel_id=1, source_target_pairs={{0,4},{4,8},{8,12},{12,16},{16,20},{20,24},{24,28},{28,32},{32,36}... | collective-permute-start | bytes 393224 | tf_op jit(solution)/shard_map/ppermute | solution.py:15
  624.7 10.8 %collective-permute-start.49 = (f32[16,2048]{1,0:T(8,128)S(1)}, f32[16,2048]{1,0:T(8,128)S(1)}, u32[]{:S(2)}, u32[]{:S(2)}) collective-permute-start(f32[16,2048]{1,0:T(8,128)S(1)} %bitcast_add_fusion.2), channel_id=1, source_target_pairs={{0,4},{4,8},{8,12},{12,16},{16,20},{20,24},{24,28},{28,32},{32,36}... | collective-permute-start | bytes 393224 | tf_op jit(solution)/shard_map/ppermute | solution.py:15
  635.5 10.8 %collective-permute-start.50 = (f32[16,2048]{1,0:T(8,128)S(1)}, f32[16,2048]{1,0:T(8,128)S(1)}, u32[]{:S(2)}, u32[]{:S(2)}) collective-permute-start(f32[16,2048]{1,0:T(8,128)S(1)} %bitcast_add_fusion.1), channel_id=1, source_target_pairs={{0,4},{4,8},{8,12},{12,16},{16,20},{20,24},{24,28},{28,32},{32,36}... | collective-permute-start | bytes 393224 | tf_op jit(solution)/shard_map/ppermute | solution.py:15
  (44 other events, 1553.9 us)
